TPU v7x, 32 devices: a whole 2x2x4 slice. The times are simulated.
32 devices in a mesh: section: 2 (over x), fsdp: 4 (over y, core), ctx: 4 (over z).
Axes of the slice: x: 2, y: 2, z: 4, core: 2. Of those that a mesh axis runs over, the one named last changes fastest.
Arguments:
- tokens: bfloat16 [2, 4096, 576], P(None, ('fsdp', 'ctx')), may hold values from -6 to 6
- cotangent: bfloat16 [2, 4096, 576], P(None, ('fsdp', 'ctx')), may hold values from -6 to 6
- doc_lengths: int32 [2, 4, 3], P(None, 'fsdp'), may hold values from 1 to 1022, as said below
- norm_gains: bfloat16 [2, 2, 576], P('section', None, ('fsdp', 'ctx')), may hold values from 0.5 to 1.5
- w_qkv: bfloat16 [2, 576, 960], P('section', ('fsdp', 'ctx')), may hold values from -0.25 to 0.25
- w_out: bfloat16 [2, 576, 576], P('section', ('fsdp', 'ctx')), may hold values from -4 to 4
- w_gate_up: bfloat16 [2, 576, 3072], P('section', ('fsdp', 'ctx')), may hold values from -0.25 to 0.25
- w_down: bfloat16 [2, 1536, 576], P('section', ('fsdp', 'ctx')), may hold values from -0.15625 to 0.15625
Outputs:
- activations: bfloat16 [2, 2, 4096, 576], P('section', None, ('fsdp', 'ctx'))
- input_grads: float32 [2, 2, 4096, 576], P('section', None, ('fsdp', 'ctx'))
- grad_attn_gains: float32 [2, 576], P('section', ('fsdp', 'ctx'))
- grad_ffn_gains: float32 [2, 576], P('section', ('fsdp', 'ctx'))
- grad_w_qkv: float32 [2, 576, 960], P('section', ('fsdp', 'ctx'))
- grad_w_out: float32 [2, 576, 576], P('section', ('fsdp', 'ctx'))
- grad_w_gate_up: float32 [2, 576, 3072], P('section', ('fsdp', 'ctx'))
- grad_w_down: float32 [2, 1536, 576], P('section', ('fsdp', 'ctx'))
Inputs may be any that keep to these rules, and one draw needn't show every extreme that they name: `doc_lengths`: each packed row holds three sequences whose lengths sum to 1024; the second one starts on the first index of ctx and ends on the last.
All inputs are finite; a program needn't handle non-finite values.
Results may differ from a plain program's by a relative error of at most 0.015.
Values may be sent and summed in bfloat16 or wider, within the bound.
A program may use at most 128 MiB of HBM per device.

v0:
```python
from functools import partial

import jax
import jax.numpy as jnp
from jax import lax
from jax.sharding import PartitionSpec as P

HEADS = 9
KV = 3
HD = 64
PACK = 1024


EPSILON = 1e-05
ROPE_BASE = 100000.0
MASKED = -1e30


def shifted(value, axis, steps):
    count = lax.axis_size(axis)
    leading, last = (max(0, -steps), min(count, count - steps))
    return lax.ppermute(value, axis, [(source, source + steps) for source in range(leading, last)])


def matmul(left_side, right_side):
    return jnp.dot(left_side, right_side, preferred_element_type=jnp.float32)


def times_transposed(left_side, right_side):
    return lax.dot_general(
        left_side, right_side, (((1,), (1,)), ((), ())), preferred_element_type=jnp.float32
    )


def transposed_times(left_side, right_side):
    return lax.dot_general(
        left_side, right_side, (((0,), (0,)), ((), ())), preferred_element_type=jnp.float32
    )


def norm_scale(values, norm_gain):
    return values * lax.rsqrt(jnp.mean(values * values, -1, keepdims=True) + EPSILON) * norm_gain


def swiglu(gate_up):
    half_width = gate_up.shape[1] // 2
    return jax.nn.silu(gate_up[:, :half_width]) * gate_up[:, half_width:]


def rotate(values, docpos):
    half_size = values.shape[-1] // 2
    frequency = ROPE_BASE ** (-(jnp.arange(half_size, dtype=jnp.float32) * 2.0 / values.shape[-1]))
    angles = docpos[:, None] * frequency[None, :]
    cosine = jnp.cos(angles)[:, None, :]
    sine_rows = jnp.sin(angles)[:, None, :]
    lower_half = values[..., :half_size]
    upper_half = values[..., half_size:]
    return jnp.concatenate(
        [
            lower_half * cosine - upper_half * sine_rows,
            upper_half * cosine + lower_half * sine_rows,
        ],
        -1,
    )


def rotate_back(grads, docpos):
    _, pullback = jax.vjp(partial(rotate, docpos=docpos), jnp.zeros(grads.shape, jnp.float32))
    return pullback(grads)[0]


def layout(lengths, pack_len):
    seq_ends = jnp.cumsum(lengths)
    starts = seq_ends - lengths
    places = jnp.arange(pack_len, dtype=jnp.int32)
    segment = jnp.sum((places[:, None] >= seq_ends[None, :2]).astype(jnp.int32), -1)
    owners = segment[:, None] == jnp.arange(3, dtype=jnp.int32)[None, :]
    begins = jnp.sum(jnp.where(owners, starts[None, :], 0), -1)
    docpos = (places - begins).astype(jnp.float32)
    return (segment, docpos)


def split_pack(pack_kv):
    pack_len = pack_kv.shape[0]
    kv_width = pack_kv.shape[1] // 2
    key_groups = jnp.transpose(pack_kv[:, :kv_width].reshape(pack_len, KV, HD), (1, 0, 2))
    value_groups = jnp.transpose(pack_kv[:, kv_width:].reshape(pack_len, KV, HD), (1, 0, 2))
    return (key_groups, value_groups)


def group_forward(operands, visible, score_scale):
    query_group, key_group, value_group = operands
    scores = (
        jnp.einsum("qgd,pd->gqp", query_group, key_group, preferred_element_type=jnp.float32)
        * score_scale
    )
    scores = jnp.where(visible[None], scores, MASKED)
    row_max = jnp.max(scores, -1, keepdims=True)
    exponent = jnp.exp(scores - row_max)
    row_sum = jnp.sum(exponent, -1, keepdims=True)
    shares = (exponent / row_sum).astype(jnp.bfloat16)
    mixed_rows = jnp.einsum("gqp,pd->qgd", shares, value_group, preferred_element_type=jnp.float32)
    return (mixed_rows, row_max + jnp.log(row_sum))


def attention_forward(queries, pack_kv, visible):
    row_count = queries.shape[0]
    groups = HEADS // KV
    query_groups = jnp.transpose(queries.reshape(row_count, KV, groups, HD), (1, 0, 2, 3))
    key_groups, value_groups = split_pack(pack_kv)
    mixed_rows, log_total = lax.map(
        partial(group_forward, visible=visible, score_scale=HD ** (-0.5)),
        (query_groups, key_groups, value_groups),
    )
    return (jnp.transpose(mixed_rows, (1, 0, 2, 3)).reshape(row_count, HEADS * HD), log_total)


def attention_skip(queries, pack_kv, visible):
    row_count = queries.shape[0]
    groups = HEADS // KV
    return (
        jnp.zeros((row_count, HEADS * HD), jnp.float32),
        jnp.zeros((KV, groups, row_count, 1), jnp.float32),
    )


def group_backward(operands, visible, score_scale):
    query_group, key_group, value_group, grad_group, log_group = operands
    scores = (
        jnp.einsum("qgd,pd->gqp", query_group, key_group, preferred_element_type=jnp.float32)
        * score_scale
    )
    scores = jnp.where(visible[None], scores, MASKED)
    shares = jnp.exp(scores - log_group)
    share_grad = jnp.einsum(
        "qgd,pd->gqp", grad_group, value_group, preferred_element_type=jnp.float32
    )
    row_dot = jnp.sum(shares * share_grad, -1, keepdims=True)
    score_grad = (shares * (share_grad - row_dot)).astype(jnp.bfloat16)
    query_grad = (
        jnp.einsum("gqp,pd->qgd", score_grad, key_group, preferred_element_type=jnp.float32)
        * score_scale
    )
    key_grad = (
        jnp.einsum("gqp,qgd->pd", score_grad, query_group, preferred_element_type=jnp.float32)
        * score_scale
    )
    value_grad = jnp.einsum(
        "gqp,qgd->pd", shares.astype(jnp.bfloat16), grad_group, preferred_element_type=jnp.float32
    )
    return (query_grad, key_grad, value_grad)


def attention_backward(queries, pack_kv, log_total, mixed_grad, visible):
    row_count = queries.shape[0]
    pack_len = pack_kv.shape[0]
    groups = HEADS // KV
    query_groups = jnp.transpose(queries.reshape(row_count, KV, groups, HD), (1, 0, 2, 3))
    grad_groups = jnp.transpose(mixed_grad.reshape(row_count, KV, groups, HD), (1, 0, 2, 3))
    key_groups, value_groups = split_pack(pack_kv)
    query_grad, key_grad, value_grad = lax.map(
        partial(group_backward, visible=visible, score_scale=HD ** (-0.5)),
        (query_groups, key_groups, value_groups, grad_groups, log_total),
    )
    query_grad = jnp.transpose(query_grad, (1, 0, 2, 3)).reshape(row_count, HEADS, HD)
    key_flat = jnp.transpose(key_grad, (1, 0, 2)).reshape(pack_len, KV * HD)
    value_flat = jnp.transpose(value_grad, (1, 0, 2)).reshape(pack_len, KV * HD)
    return (query_grad, jnp.concatenate([key_flat, value_flat], -1))


def attention_back_skip(queries, pack_kv, log_total, mixed_grad, visible):
    row_count = queries.shape[0]
    return (jnp.zeros((row_count, HEADS, HD), jnp.float32), jnp.zeros(pack_kv.shape, jnp.float32))


def layer_forward(hidden_in, lengths, weights, active, ctx_index):
    gain_pair, qkv_weight, out_weight, gate_up_weight, down_weight = weights
    row_count = hidden_in.shape[0]
    query_width = HEADS * HD
    kv_width = KV * HD
    segment, docpos = layout(lengths, PACK)
    offset = ctx_index * row_count
    local_seg = lax.dynamic_slice_in_dim(segment, offset, row_count)
    local_pos = lax.dynamic_slice_in_dim(docpos, offset, row_count)
    query_place = offset + jnp.arange(row_count, dtype=jnp.int32)
    visible = (local_seg[:, None] == segment[None, :]) & (
        query_place[:, None] >= jnp.arange(PACK, dtype=jnp.int32)[None, :]
    )
    hidden = hidden_in.astype(jnp.float32)
    normed = norm_scale(hidden, gain_pair[0].astype(jnp.float32)).astype(jnp.bfloat16)
    projected = matmul(normed, qkv_weight)
    queries = rotate(projected[:, :query_width].reshape(row_count, HEADS, HD), local_pos).astype(
        jnp.bfloat16
    )
    key_part = rotate(
        projected[:, query_width : query_width + kv_width].reshape(row_count, KV, HD), local_pos
    )
    local_kv = jnp.concatenate(
        [key_part.reshape(row_count, kv_width), projected[:, query_width + kv_width :]], -1
    ).astype(jnp.bfloat16)
    pack_kv = lax.all_gather(local_kv, "ctx", axis=0, tiled=True)
    mixed_rows, log_total = lax.cond(
        active, attention_forward, attention_skip, queries, pack_kv, visible
    )
    mixed_low = mixed_rows.astype(jnp.bfloat16)
    attended = hidden + matmul(mixed_low, out_weight)
    normed_two = norm_scale(attended, gain_pair[1].astype(jnp.float32)).astype(jnp.bfloat16)
    gate_up = matmul(normed_two, gate_up_weight)
    inner_rows = swiglu(gate_up).astype(jnp.bfloat16)
    result = attended + matmul(inner_rows, down_weight)
    saved = (
        hidden,
        normed,
        queries,
        pack_kv,
        log_total,
        mixed_low,
        attended,
        normed_two,
        gate_up,
        inner_rows,
        visible,
        local_pos,
    )
    return (result.astype(jnp.bfloat16), saved)


def layer_backward(upstream, saved, weights, active):
    gain_pair, qkv_weight, out_weight, gate_up_weight, down_weight = weights
    (
        hidden,
        normed,
        queries,
        pack_kv,
        log_total,
        mixed_low,
        attended,
        normed_two,
        gate_up,
        inner_rows,
        visible,
        local_pos,
    ) = saved
    row_count = hidden.shape[0]
    kv_width = KV * HD
    branch_grad = upstream.astype(jnp.bfloat16)
    inner_grad = times_transposed(branch_grad, down_weight)
    grad_down = transposed_times(inner_rows, branch_grad)
    gate_up_grad = jax.vjp(swiglu, gate_up)[1](inner_grad)[0].astype(jnp.bfloat16)
    normed_two_grad = times_transposed(gate_up_grad, gate_up_weight)
    grad_gate_up = transposed_times(normed_two, gate_up_grad)
    _, pull_two = jax.vjp(norm_scale, attended, gain_pair[1].astype(jnp.float32))
    attended_part, gain_two_grad = pull_two(normed_two_grad)
    attended_grad = upstream + attended_part
    out_branch = attended_grad.astype(jnp.bfloat16)
    mixed_grad = times_transposed(out_branch, out_weight).astype(jnp.bfloat16)
    grad_out = transposed_times(mixed_low, out_branch)
    query_grad, pack_kv_grad = lax.cond(
        active,
        attention_backward,
        attention_back_skip,
        queries,
        pack_kv,
        log_total,
        mixed_grad,
        visible,
    )
    local_kv_grad = lax.psum_scatter(
        pack_kv_grad.astype(jnp.bfloat16), "ctx", scatter_dimension=0, tiled=True
    ).astype(jnp.float32)
    query_pre = rotate_back(query_grad, local_pos).reshape(row_count, HEADS * HD)
    key_pre = rotate_back(
        local_kv_grad[:, :kv_width].reshape(row_count, KV, HD), local_pos
    ).reshape(row_count, kv_width)
    projected_grad = jnp.concatenate([query_pre, key_pre, local_kv_grad[:, kv_width:]], -1).astype(
        jnp.bfloat16
    )
    normed_grad = times_transposed(projected_grad, qkv_weight)
    grad_qkv = transposed_times(normed, projected_grad)
    _, pull_one = jax.vjp(norm_scale, hidden, gain_pair[0].astype(jnp.float32))
    hidden_part, gain_one_grad = pull_one(normed_grad)
    input_grad = attended_grad + hidden_part
    return (input_grad, (gain_one_grad, gain_two_grad, grad_qkv, grad_out, grad_gate_up, grad_down))


def on_device(tokens, cotangent, doc_lengths, norm_gains, w_qkv, w_out, w_gate_up, w_down):
    section_index = lax.axis_index("section")
    ctx_index = lax.axis_index("ctx")
    micro_count = tokens.shape[0]
    row_count = tokens.shape[1]
    width = tokens.shape[2]
    tick_count = micro_count + 1
    shards = (norm_gains, w_qkv, w_out, w_gate_up, w_down)
    gathered = (
        lax.all_gather(shards[0], ("fsdp", "ctx"), axis=2, tiled=True),
        lax.all_gather(shards[1], ("fsdp", "ctx"), axis=1, tiled=True),
        lax.all_gather(shards[2], ("fsdp", "ctx"), axis=1, tiled=True),
        lax.all_gather(shards[3], ("fsdp", "ctx"), axis=1, tiled=True),
        lax.all_gather(shards[4], ("fsdp", "ctx"), axis=1, tiled=True),
    )
    weights = tuple((member[0] for member in gathered))
    incoming = jnp.zeros((row_count, width), jnp.bfloat16)
    outputs = []
    saved_ticks = []
    for tick_index in range(tick_count):
        first_input = tokens[min(tick_index, micro_count - 1)]
        hidden_in = jnp.where(section_index == 0, first_input, incoming)
        micro_index = tick_index - section_index
        active = (micro_index >= 0) & (micro_index < micro_count)
        lengths = lax.dynamic_index_in_dim(
            doc_lengths, jnp.clip(micro_index, 0, micro_count - 1), 0, keepdims=False
        )[0]
        result, saved = layer_forward(hidden_in, lengths, weights, active, ctx_index)
        outputs.append(result)
        saved_ticks.append(saved)
        if tick_index < micro_count:
            incoming = shifted(result, "section", 1)
    regathered = (
        lax.all_gather(shards[0], ("fsdp", "ctx"), axis=2, tiled=True),
        lax.all_gather(shards[1], ("fsdp", "ctx"), axis=1, tiled=True),
        lax.all_gather(shards[2], ("fsdp", "ctx"), axis=1, tiled=True),
        lax.all_gather(shards[3], ("fsdp", "ctx"), axis=1, tiled=True),
        lax.all_gather(shards[4], ("fsdp", "ctx"), axis=1, tiled=True),
    )
    back_weights = tuple((member[0] for member in regathered))
    totals = None
    incoming_grad = jnp.zeros((row_count, width), jnp.bfloat16)
    input_grads = []
    for tick_index in range(tick_count):
        forward_tick = micro_count - tick_index
        upstream_given = cotangent[max(micro_count - 1 - tick_index, 0)].astype(jnp.float32)
        upstream = jnp.where(section_index == 1, upstream_given, incoming_grad.astype(jnp.float32))
        micro_index = forward_tick - section_index
        active = (micro_index >= 0) & (micro_index < micro_count)
        input_grad, weight_grads = layer_backward(
            upstream, saved_ticks[forward_tick], back_weights, active
        )
        factor = active.astype(jnp.float32)
        weight_grads = tuple((member * factor for member in weight_grads))
        totals = (
            weight_grads
            if totals is None
            else tuple((running + newest for running, newest in zip(totals, weight_grads)))
        )
        input_grads.append(input_grad)
        if tick_index < micro_count:
            incoming_grad = shifted(input_grad.astype(jnp.bfloat16), "section", -1)
    shaped = tuple((member[None] for member in totals))
    totals = (
        lax.psum_scatter(shaped[0], ("fsdp", "ctx"), scatter_dimension=1, tiled=True),
        lax.psum_scatter(shaped[1], ("fsdp", "ctx"), scatter_dimension=1, tiled=True),
        lax.psum_scatter(shaped[2], ("fsdp", "ctx"), scatter_dimension=1, tiled=True),
        lax.psum_scatter(shaped[3], ("fsdp", "ctx"), scatter_dimension=1, tiled=True),
        lax.psum_scatter(shaped[4], ("fsdp", "ctx"), scatter_dimension=1, tiled=True),
        lax.psum_scatter(shaped[5], ("fsdp", "ctx"), scatter_dimension=1, tiled=True),
    )
    stacked_out = jnp.stack(outputs)
    activations = lax.dynamic_slice_in_dim(stacked_out, section_index, micro_count, 0)[None]
    stacked_grad = jnp.stack(input_grads)[::-1]
    grads_out = lax.dynamic_slice_in_dim(stacked_grad, section_index, micro_count, 0)[None]
    return (activations, grads_out) + tuple(totals)


def solution(mesh):
    return jax.shard_map(
        on_device,
        mesh=mesh,
        in_specs=(
            P(None, ("fsdp", "ctx"), None),
            P(None, ("fsdp", "ctx"), None),
            P(None, "fsdp", None),
            P("section", None, ("fsdp", "ctx")),
            P("section", ("fsdp", "ctx"), None),
            P("section", ("fsdp", "ctx"), None),
            P("section", ("fsdp", "ctx"), None),
            P("section", ("fsdp", "ctx"), None),
        ),
        out_specs=(
            P("section", None, ("fsdp", "ctx"), None),
            P("section", None, ("fsdp", "ctx"), None),
            P("section", ("fsdp", "ctx")),
            P("section", ("fsdp", "ctx")),
            P("section", ("fsdp", "ctx"), None),
            P("section", ("fsdp", "ctx"), None),
            P("section", ("fsdp", "ctx"), None),
            P("section", ("fsdp", "ctx"), None),
        ),
        check_vma=False,
    )
```

profile of v0, /device:TPU:0, one launch (start us, length us, event | category | flops | bytes accessed | tf_op | source)
XLA Modules:
  0.0 816.6 jit_solution(1652424681836923153)
XLA Ops:
  16.9 62.8 %all_gather.32 = bf16[1,576,576]{2,0,1:T(2,128)(2,1)S(1)} all-gather(bf16[1,36,576]{2,0,1:T(2,128)(2,1)S(1)} %copy.88), channel_id=1, replica_groups=mesh['section'=2,'fsdp'=4,'ctx'=4] {'fsdp','ctx'}, dimensions={1}, use_global_device_ids=true | all-gather | bytes 705024 | tf_op jit(solution)/shard_map/all_gather | solution.py:297
  81.2 36.8 %all_gather.29 = bf16[1,2,576]{1,0,2:T(2,128)(2,1)S(1)} all-gather(bf16[1,2,36]{1,0,2:T(2,128)(2,1)S(1)} %copy.86), channel_id=1, replica_groups=mesh['section'=2,'fsdp'=4,'ctx'=4] {'fsdp','ctx'}, dimensions={2}, use_global_device_ids=true | all-gather | bytes 2448 | tf_op jit(solution)/shard_map/all_gather | solution.py:295
  126.9 21.3 %all_gather.31 = bf16[1024,384]{0,1:T(8,128)(2,1)} all-gather(bf16[256,384]{0,1:T(8,128)(2,1)S(1)} %pad_maximum_fusion.16), channel_id=1, replica_groups=mesh['section'=2,'fsdp'=4,'ctx'=4] {'ctx'}, dimensions={0}, use_global_device_ids=true | all-gather | bytes 983040 | tf_op jit(solution)/shard_map/all_gather | solution.py:201
  148.2 15.3 %conditional.6 = (f32[3,3,256,1]{2,1,3,0:T(4,128)}, bf16[256,576]{0,1:T(8,128)(2,1)}) conditional(s32[]{:T(128)} %convert_element_type.278, () %tuple.108, (bf16[256,9,64]{0,2,1:T(8,128)(2,1)}, bf16[1024,384]{0,1:T(8,128)(2,1)}, pred[256,1024]{0,1:T(8,128)(4,1)S(1)}) %tuple.109), branch_computations={%region_4.5_spmd, %region_5.10_spmd} | conditional | flops 210763008 | bytes 12383417 | solution.py:202
  149.4 14.0 %while.87 = (s32[]{:T(128)}, bf16[3,256,3,64]{1,3,2,0:T(8,128)(2,1)}, f32[3,3,256,1]{2,1,3,0:T(4,128)}, bf16[3,1024,64]{1,2,0:T(8,128)(2,1)S(1)}, pred[256,1024]...) while((s32[]{:T(128)}, ...), condition=%wide.region_9.9_spmd, body=%wide.region_6.8_spmd.sunk | while | flops 210763008 | bytes 10810465 | solution.py:111
  175.3 7.0 all-gather.8.cloned.1.call-done
  189.9 6.3 collective-permute-done
  200.2 18.6 %all_gather.35 = bf16[1024,384]{0,1:T(8,128)(2,1)} all-gather(bf16[256,384]{0,1:T(8,128)(2,1)S(1)} %pad_maximum_fusion.17), channel_id=1, replica_groups=mesh['section'=2,'fsdp'=4,'ctx'=4] {'ctx'}, dimensions={0}, use_global_device_ids=true | all-gather | bytes 983040 | tf_op jit(solution)/shard_map/all_gather | solution.py:201
  219.6 19.3 %conditional.7 = (f32[3,3,256,1]{2,1,3,0:T(4,128)}, bf16[256,576]{0,1:T(8,128)(2,1)}) conditional(s32[]{:T(128)} %convert_element_type.292, () %tuple.110, (bf16[256,9,64]{0,2,1:T(8,128)(2,1)}, bf16[1024,384]{0,1:T(8,128)(2,1)}, pred[256,1024]{0,1:T(8,128)(4,1)}) %tuple.111), branch_computations={%region_15.16_spmd, %region_16.21_spmd} | conditional | flops 210763008 | bytes 13429973 | solution.py:202
  221.6 17.2 %while.88 = (s32[]{:T(128)}, bf16[3,256,3,64]{1,3,2,0:T(8,128)(2,1)}, f32[3,3,256,1]{2,1,3,0:T(4,128)}, bf16[3,1024,64]{1,2,0:T(8,128)(2,1)}, pred[256,1024]{0,1...) while((s32[]{:T(128)}, ...), condition=%wide.region_20.20_spmd, body=%wide.region_17.19_spmd.sunk | while | flops 210763008 | bytes 11857021 | solution.py:111
  247.1 5.6 collective-permute-start.1
  260.1 17.4 %all_gather.36 = bf16[1024,384]{0,1:T(8,128)(2,1)} all-gather(bf16[256,384]{0,1:T(8,128)(2,1)S(1)} %pad_maximum_fusion.18), channel_id=1, replica_groups=mesh['section'=2,'fsdp'=4,'ctx'=4] {'ctx'}, dimensions={0}, use_global_device_ids=true | all-gather | bytes 983040 | tf_op jit(solution)/shard_map/all_gather | solution.py:201
  300.7 61.0 %reduce-scatter.6.cloned.1.call-done = bf16[256,384]{0,1:T(8,128)(2,1)} async-done(((bf16[1024,384]{0,1:T(8,128)(2,1)}), bf16[256,384]{0,1:T(8,128)(2,1)}) %reduce-scatter.6.cloned.1.call-update) | async-done | bytes 196624 | tf_op jit(solution)/shard_map/reduce_scatter | solution.py:268
  371.3 5.6 collective-permute-done.2
  382.4 30.1 %conditional.10 = (bf16[1024,384]{0,1:T(8,128)(2,1)}, f32[256,9,32]{0,2,1:T(8,128)}, f32[256,9,32]{0,2,1:T(8,128)}, f32[256,9,32]{0,2,1:T(8,128)}) conditional(s32[]{:T(128)} %convert_element_type.292, () %tuple.116, (bf16[256,9,64]{0,2,1:T(8,128)(2,1)}, bf16[1024,384]{0,1:T(8,128)(2,1)}, bf16[256,576]{0,1:T(8,128)(2,1)}, ...), branch_computations={%region_42.43_spmd, %region_43.47_spmd} | conditional | flops 512154880 | bytes 40097212 | solution.py:258
  384.4 24.0 %while.91 = (s32[]{:T(128)}, f32[3,256,3,64]{1,3,2,0:T(8,128)}, bf16[3,1024,64]{1,2,0:T(8,128)(2,1)}, bf16[3,1024,64]{1,2,0:T(8,128)(2,1)}, bf16[3,1024,64]{1,2,...) while((s32[]{:T(128)}, f32[3,256,3,64]{1,3,2,0:T(8,128)}, ...), condition=%wide.region_46.46_spmd, body=%wide.region_44.45_spmd.sunk | while | flops 510508288 | bytes 35476796 | solution.py:161
  426.7 8.7 %reduce-scatter.8.cloned.1.call-done = bf16[256,384]{0,1:T(8,128)(2,1)} async-done(((bf16[1024,384]{0,1:T(8,128)(2,1)}), bf16[256,384]{0,1:T(8,128)(2,1)}) %reduce-scatter.8.cloned.1.call-update) | async-done | bytes 196624 | tf_op jit(solution)/shard_map/reduce_scatter | solution.py:268
  455.1 28.6 %conditional.11 = (bf16[1024,384]{0,1:T(8,128)(2,1)}, f32[256,9,32]{0,2,1:T(8,128)S(1)}, f32[256,9,32]{0,2,1:T(8,128)}, f32[256,9,32]{0,2,1:T(8,128)}) conditional(s32[]{:T(128)} %convert_element_type.278, () %tuple.118, (bf16[256,9,64]{0,2,1:T(8,128)(2,1)}, bf16[1024,384]{0,1:T(8,128)(2,1)}, bf16[256,576]{0,1:T(8,128)(2,1)S(1)}, ...), branch_computations={%region_50.51_spmd, %region_51.55_spmd} | conditional | flops 512154880 | bytes 36296040 | solution.py:258
  456.4 23.2 %while.92 = (s32[]{:T(128)}, f32[3,256,3,64]{1,3,2,0:T(8,128)}, bf16[3,1024,64]{1,2,0:T(8,128)(2,1)}, bf16[3,1024,64]{1,2,0:T(8,128)(2,1)}, bf16[3,1024,64]{1,2,...) while((s32[]{:T(128)}, f32[3,256,3,64]{1,3,2,0:T(8,128)}, ...), condition=%wide.region_54.54_spmd, body=%wide.region_52.53_spmd.sunk | while | flops 510508288 | bytes 31675624 | solution.py:161
  488.5 6.1 add_bitcast_fusion
  494.7 20.9 %copy.92 = f32[1,576,3072]{2,0,1:T(1,128)} copy(f32[1,576,3072]{2,1,0:T(8,128)S(1)} %add_bitcast_fusion) | data formatting | bytes 14155776 | tf_op jit(solution)/shard_map/broadcast_in_dim | solution.py:348
  516.4 5.9 copy.93
  540.4 36.0 %all-reduce.24 = (f32[1,576]{1,0:T(1,128)S(1)}, f32[1,576]{1,0:T(1,128)S(1)}) all-reduce(f32[1,576]{1,0:T(1,128)S(1)} %add.386, f32[1,576]{1,0:T(1,128)S(1)} %add.389), channel_id=5, replica_groups=mesh['section'=2,'fsdp'=4,'ctx'=4] {'fsdp','ctx'}, use_global_device_ids=true, to_apply=%region_60.61.clone | all-reduce | flops 1152 | bytes 9216
  578.6 224.1 %all-reduce.28.cloned.1.call-done = (f32[1,576,960]{2,0,1:T(1,128)}, f32[1,576,576]{2,0,1:T(1,128)}, f32[1,576,3072]{2,0,1:T(1,128)}, f32[1,1536,576]{2,0,1:T(1,128)}) async-done(((f32[1,576,960]{2,0,1:T(1,128)}, f32[1,576,576]{2,0,1:T(1,128)}, f32[1,576,3072]{2,0,1:T(1,128)}, f32[1,1536,576]{2,0,1:T(1,128)}), (f32[1,576,960]{2,0,1:T(1,128)}, f32[1,576,576]{2,0,1:T(1,128)}, f32[1,576,3072]{2,0,1:T(1,128)}, ...) | async-done | bytes 14155792
  (562 shorter events, 259.0 us)
Async XLA Ops:
  7.2 73.8 %copy-start.130 = (bf16[1,2,36]{2,1,0:T(2,128)(2,1)S(1)}, bf16[1,2,36]{2,1,0:T(2,128)(2,1)}, u32[]{:S(2)}) copy-start(bf16[1,2,36]{2,1,0:T(2,128)(2,1)} %param.35) | copy-start | bytes 436
  7.2 115.6 %all-gather.4.cloned.1.call-start = ((), (), s32[]{:S(2)}) async-start(), calls=%async_computation.3 | async-start | bytes 2506752 | tf_op jit(solution)/shard_map/all_gather | solution.py:296
  8.9 157.5 %all-gather.6.cloned.1.call-start = ((), (), s32[]{:S(2)}) async-start(), calls=%async_computation.4 | async-start | bytes 7520256 | tf_op jit(solution)/shard_map/all_gather | solution.py:298
  11.0 171.3 %all-gather.8.cloned.1.call-start = ((), (), s32[]{:S(2)}) async-start(), calls=%async_computation.5 | async-start | bytes 2088960 | tf_op jit(solution)/shard_map/all_gather | solution.py:299
  11.8 349.9 %reduce-scatter.6.cloned.1.call-start = ((), (), s32[]{:S(2)}) async-start(), calls=%async_computation.6 | async-start | bytes 983040 | tf_op jit(solution)/shard_map/reduce_scatter | solution.py:268
  15.0 110.1 %copy-start.108 = (f32[256]{0:T(256)}, f32[256]{0:T(256)S(1)}, u32[]{:S(2)}) copy-start(f32[256]{0:T(256)S(1)} %fusion.319) | copy-start | bytes 3076
  80.7 45.3 %copy-start.80 = (f32[256,32]{0,1:T(8,128)}, f32[256,32]{0,1:T(8,128)S(1)}, u32[]{:S(2)}) copy-start(f32[256,32]{0,1:T(8,128)S(1)} %get-tuple-element.692) | copy-start | bytes 98308
  80.7 45.3 %copy-start.82 = (f32[256,32]{0,1:T(8,128)}, f32[256,32]{0,1:T(8,128)S(1)}, u32[]{:S(2)}) copy-start(f32[256,32]{0,1:T(8,128)S(1)} %get-tuple-element.693) | copy-start | bytes 98308
  81.2 82.3 %copy-start.6 = (bf16[1,576,576]{2,1,0:T(8,128)(2,1)}, bf16[1,576,576]{2,1,0:T(8,128)(2,1)S(1)}, u32[]{:S(2)}) copy-start(bf16[1,576,576]{2,1,0:T(8,128)(2,1)S(1)} %copy.112) | copy-start | bytes 1990660
  122.8 25.4 %copy-start = (pred[256,1024]{0,1:T(8,128)(4,1)}, pred[256,1024]{0,1:T(8,128)(4,1)S(1)}, u32[]{:S(2)}) copy-start(pred[256,1024]{0,1:T(8,128)(4,1)S(1)} %get-tuple-element.683) | copy-start | bytes 786436
  185.8 10.4 %collective-permute-start = (bf16[256,576]{0,1:T(8,128)(2,1)}, bf16[256,576]{0,1:T(8,128)(2,1)}, u32[]{:S(2)}, u32[]{:S(2)}) collective-permute-start(bf16[256,576]{0,1:T(8,128)(2,1)} %fusion.210), channel_id=1, source_target_pairs={{0,16},{1,17},{2,18},{3,19},{4,20},{5,21},{6,22},{7,23},{8,24},{9,... | collective-permute-start | bytes 884744 | tf_op jit(solution)/shard_map/ppermute | solution.py:22
  247.1 9.0 %collective-permute-start.1 = (bf16[256,576]{0,1:T(8,128)(2,1)}, bf16[256,576]{0,1:T(8,128)(2,1)}, u32[]{:S(2)}, u32[]{:S(2)}) collective-permute-start(bf16[256,576]{0,1:T(8,128)(2,1)} %fusion.207), channel_id=1, source_target_pairs={{0,16},{1,17},{2,18},{3,19},{4,20},{5,21},{6,22},{7,23},{8,24},{9,... | collective-permute-start | bytes 884744 | tf_op jit(solution)/shard_map/ppermute | solution.py:22
  292.9 142.5 %reduce-scatter.8.cloned.1.call-start = ((), (), s32[]{:S(2)}) async-start(), calls=%async_computation.7 | async-start | bytes 983040 | tf_op jit(solution)/shard_map/reduce_scatter | solution.py:268
  367.5 9.5 %collective-permute-start.2 = (bf16[256,576]{0,1:T(8,128)(2,1)S(1)}, bf16[256,576]{0,1:T(8,128)(2,1)S(1)}, u32[]{:S(2)}, u32[]{:S(2)}) collective-permute-start(bf16[256,576]{0,1:T(8,128)(2,1)S(1)} %get-tuple-element.642), channel_id=1, source_target_pairs={{16,0},{17,1},{18,2},{19,3},{20,4},{21,5},{22,6},{23,7},{24,8},{25... | collective-permute-start | bytes 884744 | tf_op jit(solution)/shard_map/ppermute | solution.py:22
  412.5 111.2 %reduce-scatter.10.cloned.1.call-start = ((), (), s32[]{:S(2)}) async-start(), calls=%async_computation.8 | async-start | bytes 983040 | tf_op jit(solution)/shard_map/reduce_scatter | solution.py:268
  441.0 9.6 %collective-permute-start.3 = (bf16[256,576]{0,1:T(8,128)(2,1)S(1)}, bf16[256,576]{0,1:T(8,128)(2,1)S(1)}, u32[]{:S(2)}, u32[]{:S(2)}) collective-permute-start(bf16[256,576]{0,1:T(8,128)(2,1)S(1)} %get-tuple-element.644), channel_id=1, source_target_pairs={{16,0},{17,1},{18,2},{19,3},{20,4},{21,5},{22,6},{23,7},{24,8},{25... | collective-permute-start | bytes 884744 | tf_op jit(solution)/shard_map/ppermute | solution.py:22
  454.7 29.1 %copy-start.32 = (f32[256,576]{0,1:T(8,128)}, f32[256,576]{0,1:T(8,128)S(1)}, u32[]{:S(2)}) copy-start(f32[256,576]{0,1:T(8,128)S(1)} %fusion.261) | copy-start | bytes 1769476
  455.1 28.7 %copy-start.49 = (f32[576,576]{1,0:T(8,128)S(1)}, f32[576,576]{1,0:T(8,128)}, u32[]{:S(2)}) copy-start(f32[576,576]{1,0:T(8,128)} %fusion.304) | copy-start | bytes 3981316
  483.7 319.0 %all-reduce.28.cloned.1.call-start = ((), (), s32[]{:S(2)}) async-start(), calls=%async_computation.9 | async-start | bytes 29687808
  494.6 21.0 %copy-start.23 = (f32[1536,576]{0,1:T(8,128)S(1)}, f32[1536,576]{0,1:T(8,128)}, u32[]{:S(2)}) copy-start(f32[1536,576]{0,1:T(8,128)} %fusion.276) | copy-start | bytes 10616836
  494.6 21.0 %copy-start.24 = (f32[1536,576]{0,1:T(8,128)S(1)}, f32[1536,576]{0,1:T(8,128)}, u32[]{:S(2)}) copy-start(f32[1536,576]{0,1:T(8,128)} %fusion.313) | copy-start | bytes 10616836
  494.6 20.9 %copy-start.46 = (bf16[256,1536]{1,0:T(8,128)(2,1)S(1)}, bf16[256,1536]{1,0:T(8,128)(2,1)}, u32[]{:S(2)}) copy-start(bf16[256,1536]{1,0:T(8,128)(2,1)} %multiply_convert_fusion.2) | copy-start | bytes 2359300
  494.6 20.9 %copy-start.56 = (bf16[2,256,576]{1,2,0:T(8,128)(2,1)S(1)}, bf16[2,256,576]{1,2,0:T(8,128)(2,1)}, u32[]{:S(2)}) copy-start(bf16[2,256,576]{1,2,0:T(8,128)(2,1)} %param.33) | copy-start | bytes 1769476
  494.6 20.9 %copy-start.74 = (bf16[256,576]{0,1:T(8,128)(2,1)S(1)}, bf16[256,576]{0,1:T(8,128)(2,1)}, u32[]{:S(2)}) copy-start(bf16[256,576]{0,1:T(8,128)(2,1)} %copy-done.73) | copy-start | bytes 884740
  (135 other events, 406.0 us)
Sparse Core Ops, SparseCore 0:
  10.9 53.9 all-gather.3
  67.8 72.7 all-gather.5
  142.9 39.3 all-gather.7
  293.0 68.6 reduce-scatter.5
  412.7 22.6 reduce-scatter.7
  483.8 22.6 reduce-scatter.9
  531.1 271.5 all-reduce.27
where the time goes:
time: 826 us; the launch traced here: 817 us
  waiting for transfers between devices  320 us (39%)
  blocking collectives  193 us (23%)
  matrix products  134 us (16%)
  local copies, waits for them, and re-layouts  91.2 us (11%)
  other arithmetic  47.1 us (6%)
  between operations  17.5 us (2%)
  starting transfers between devices  13.3 us (2%)
    unnamed x8, waiting for transfers between devices  225 us
    reduce_scatter x3, waiting for transfers between devices, layer_backward(): lax.psum_scatter(pack_kv_grad.astype(jnp.bfloat16), 'ctx', scatter_dimens...  69.7 us
    all_gather x1, blocking collectives, on_device(): lax.all_gather(shards[2], ('fsdp', 'ctx'), axis=1, tiled=True)  62.8 us
    all_gather x3, blocking collectives, layer_forward(): pack_kv = lax.all_gather(local_kv, 'ctx', axis=0, tiled=True)  57.3 us
    all_gather x1, blocking collectives, on_device(): lax.all_gather(shards[0], ('fsdp', 'ctx'), axis=2, tiled=True)  36.8 us
    unnamed x1, blocking collectives  36 us
    dot_general x12, matrix products, transposed_times(): lax.dot_general(left_side, right_side, (((0,), (0,)), ((), ())), preferre...  34.8 us
    broadcast_in_dim x4, local copies, waits for them, and re-layouts, on_device(): shaped = tuple((member[None] for member in totals))  33.3 us
  transfers between devices with their start and end apart: 11, of which 8 were waited for; matrix products, arithmetic and copies ran while one was open for 14% of the time, Pallas kernels for 0%

commit v1 on v0

v1 whole, which is shorter than its diff:
```python
from functools import partial

import jax
import jax.numpy as jnp
from jax import lax
from jax.experimental import pallas as pl
from jax.experimental.pallas import tpu as pltpu
from jax.sharding import PartitionSpec as P

HEADS = 9
KV = 3
HD = 64
PACK = 1024


EPSILON = 1e-05
ROPE_BASE = 100000.0
MASKED = -1e30


def shifted(value, axis, steps):
    count = lax.axis_size(axis)
    leading, last = (max(0, -steps), min(count, count - steps))
    return lax.ppermute(value, axis, [(source, source + steps) for source in range(leading, last)])


def matmul(left_side, right_side):
    return jnp.dot(left_side, right_side, preferred_element_type=jnp.float32)


def times_transposed(left_side, right_side):
    return lax.dot_general(
        left_side, right_side, (((1,), (1,)), ((), ())), preferred_element_type=jnp.float32
    )


def transposed_times(left_side, right_side):
    return lax.dot_general(
        left_side, right_side, (((0,), (0,)), ((), ())), preferred_element_type=jnp.float32
    )


def norm_scale(values, norm_gain):
    return values * lax.rsqrt(jnp.mean(values * values, -1, keepdims=True) + EPSILON) * norm_gain


def swiglu(gate_up):
    half_width = gate_up.shape[1] // 2
    return jax.nn.silu(gate_up[:, :half_width]) * gate_up[:, half_width:]


def rotate(values, docpos):
    half_size = values.shape[-1] // 2
    frequency = ROPE_BASE ** (-(jnp.arange(half_size, dtype=jnp.float32) * 2.0 / values.shape[-1]))
    angles = docpos[:, None] * frequency[None, :]
    cosine = jnp.cos(angles)[:, None, :]
    sine_rows = jnp.sin(angles)[:, None, :]
    lower_half = values[..., :half_size]
    upper_half = values[..., half_size:]
    return jnp.concatenate(
        [
            lower_half * cosine - upper_half * sine_rows,
            upper_half * cosine + lower_half * sine_rows,
        ],
        -1,
    )


def rotate_back(grads, docpos):
    _, pullback = jax.vjp(partial(rotate, docpos=docpos), jnp.zeros(grads.shape, jnp.float32))
    return pullback(grads)[0]


def layout(lengths, pack_len):
    seq_ends = jnp.cumsum(lengths)
    starts = seq_ends - lengths
    places = jnp.arange(pack_len, dtype=jnp.int32)
    segment = jnp.sum((places[:, None] >= seq_ends[None, :2]).astype(jnp.int32), -1)
    owners = segment[:, None] == jnp.arange(3, dtype=jnp.int32)[None, :]
    begins = jnp.sum(jnp.where(owners, starts[None, :], 0), -1)
    docpos = (places - begins).astype(jnp.float32)
    return (segment, docpos)


MESH = pl.DeviceIdType.MESH
VMEM_LIMIT = 56 * 1024 * 1024


def flip(index, bit):
    return index + bit * (1 - 2 * ((index // bit) % 2))


def bits_of(count):
    bit, found = 1, []
    while bit < count:
        found.append(bit)
        bit *= 2
    return found


def meet(fsdp_me, ctx_me, fsdp_count, ctx_count):
    barrier = pltpu.get_barrier_semaphore()
    for bit in bits_of(fsdp_count):
        pl.semaphore_signal(
            barrier, inc=1, device_id={"fsdp": flip(fsdp_me, bit)}, device_id_type=MESH
        )
    for step in range(1, ctx_count):
        pl.semaphore_signal(
            barrier, inc=1, device_id={"ctx": (ctx_me + step) % ctx_count}, device_id_type=MESH
        )
    pl.semaphore_wait(barrier, len(bits_of(fsdp_count)) + ctx_count - 1)


def gather_kernel(fsdp_count, ctx_count, chunk_count, *refs):
    shards = refs[:chunk_count]
    fulls = refs[chunk_count : 2 * chunk_count]
    local_sem, send_sem, recv_sem = refs[2 * chunk_count :]
    fsdp_me, ctx_me = lax.axis_index("fsdp"), lax.axis_index("ctx")
    bits = bits_of(fsdp_count)[::-1]
    stage_count = 1 + len(bits)

    def copies(chunk, stage):
        full = fulls[chunk]
        if stage == 0:
            return [
                pltpu.make_async_remote_copy(
                    src_ref=shards[chunk],
                    dst_ref=full.at[fsdp_me, ctx_me],
                    send_sem=send_sem.at[chunk, step - 1],
                    recv_sem=recv_sem.at[chunk, step - 1],
                    device_id={"ctx": (ctx_me + step) % ctx_count},
                    device_id_type=MESH,
                )
                for step in range(1, ctx_count)
            ]
        bit = bits[stage - 1]
        first = ctx_count - 1 + sum(fsdp_count // (2 * other) for other in bits[: stage - 1])
        made = []
        for high in range(fsdp_count // (2 * bit)):
            run = fsdp_me % (2 * bit) + high * 2 * bit
            made.append(
                pltpu.make_async_remote_copy(
                    src_ref=full.at[run],
                    dst_ref=full.at[run],
                    send_sem=send_sem.at[chunk, first + high],
                    recv_sem=recv_sem.at[chunk, first + high],
                    device_id={"fsdp": flip(fsdp_me, bit)},
                    device_id_type=MESH,
                )
            )
        return made

    own = [
        pltpu.make_async_copy(
            shards[chunk], fulls[chunk].at[fsdp_me, ctx_me], local_sem.at[chunk]
        )
        for chunk in range(chunk_count)
    ]
    for copy in own:
        copy.start()
    meet(fsdp_me, ctx_me, fsdp_count, ctx_count)
    for turn in range(chunk_count + stage_count):
        for chunk in range(chunk_count):
            stage = turn - chunk
            if stage < 0 or stage > stage_count:
                continue
            if stage == 1:
                own[chunk].wait()
            if stage >= 1:
                for copy in copies(chunk, stage - 1):
                    copy.wait_recv()
            if stage < stage_count:
                for copy in copies(chunk, stage):
                    copy.start()
    for chunk in range(chunk_count):
        for stage in range(stage_count):
            for copy in copies(chunk, stage):
                copy.wait_send()


def gather_shards(shards, fsdp_count, ctx_count):
    chunk_count = len(shards)
    slots = ctx_count - 1 + fsdp_count - 1
    return pl.pallas_call(
        partial(gather_kernel, fsdp_count, ctx_count, chunk_count),
        out_shape=[
            jax.ShapeDtypeStruct((fsdp_count, ctx_count) + shard.shape, shard.dtype)
            for shard in shards
        ],
        in_specs=[pl.BlockSpec(memory_space=pl.ANY)] * chunk_count,
        out_specs=[pl.BlockSpec(memory_space=pl.ANY)] * chunk_count,
        scratch_shapes=[
            pltpu.SemaphoreType.DMA((chunk_count,)),
            pltpu.SemaphoreType.DMA((chunk_count, slots)),
            pltpu.SemaphoreType.DMA((chunk_count, slots)),
        ],
        compiler_params=pltpu.CompilerParams(collective_id=0, has_side_effects=True),
        name="gather_weights",
    )(*shards)


def reduce_kernel(fsdp_count, ctx_count, chunk_count, *refs):
    bits = bits_of(fsdp_count)
    level_count = len(bits)
    parts = refs[:chunk_count]
    outs = refs[chunk_count : 2 * chunk_count]
    scratch = refs[2 * chunk_count :]
    per_chunk = 2 * level_count + 1
    send_sem, recv_sem = scratch[chunk_count * per_chunk :]
    fsdp_me, ctx_me = lax.axis_index("fsdp"), lax.axis_index("ctx")

    def level(chunk, index):
        return parts[chunk] if index == 0 else scratch[chunk * per_chunk + 2 * index - 1]

    def landing(chunk, index):
        return scratch[chunk * per_chunk + 2 * index]

    def copies(chunk, stage):
        source = level(chunk, stage)
        if stage == level_count:
            return [
                pltpu.make_async_remote_copy(
                    src_ref=source.at[0, (ctx_me + step) % ctx_count],
                    dst_ref=landing(chunk, stage).at[step - 1],
                    send_sem=send_sem.at[chunk, fsdp_count - 1 + step - 1],
                    recv_sem=recv_sem.at[chunk, fsdp_count - 1 + step - 1],
                    device_id={"ctx": (ctx_me + step) % ctx_count},
                    device_id_type=MESH,
                )
                for step in range(1, ctx_count)
            ]
        bit = bits[stage]
        first = sum(fsdp_count // (2 * other) for other in bits[:stage])
        mine = (fsdp_me // bit) % 2
        return [
            pltpu.make_async_remote_copy(
                src_ref=source.at[1 - mine + 2 * high],
                dst_ref=landing(chunk, stage).at[high],
                send_sem=send_sem.at[chunk, first + high],
                recv_sem=recv_sem.at[chunk, first + high],
                device_id={"fsdp": flip(fsdp_me, bit)},
                device_id_type=MESH,
            )
            for high in range(fsdp_count // (2 * bit))
        ]

    def absorb(chunk, stage):
        source, landed = level(chunk, stage), landing(chunk, stage)
        if stage == level_count:
            total = source[0, ctx_me].astype(jnp.float32)
            for step in range(1, ctx_count):
                total = total + landed[step - 1].astype(jnp.float32)
            outs[chunk][...] = total
            return
        mine = (fsdp_me // bits[stage]) % 2
        target = level(chunk, stage + 1)
        for high in range(fsdp_count // (2 * bits[stage])):

            def add(place, carry):
                total = source[mine + 2 * high, place].astype(jnp.float32) + landed[
                    high, place
                ].astype(jnp.float32)
                target[high, place] = total.astype(jnp.bfloat16)
                return carry

            lax.fori_loop(0, ctx_count, add, 0)

    meet(fsdp_me, ctx_me, fsdp_count, ctx_count)
    for turn in range(chunk_count + level_count + 1):
        for chunk in range(chunk_count):
            stage = turn - chunk
            if stage < 0 or stage > level_count + 1:
                continue
            if stage >= 1:
                for copy in copies(chunk, stage - 1):
                    copy.wait_recv()
                absorb(chunk, stage - 1)
            if stage <= level_count:
                for copy in copies(chunk, stage):
                    copy.start()
    for chunk in range(chunk_count):
        for stage in range(level_count + 1):
            for copy in copies(chunk, stage):
                copy.wait_send()


def reduce_parts(parts, fsdp_count, ctx_count):
    chunk_count = len(parts)
    slots = ctx_count - 1 + fsdp_count - 1
    scratch = []
    for part in parts:
        shard = part.shape[2:]
        for bit in bits_of(fsdp_count):
            half = (fsdp_count // (2 * bit), ctx_count) + shard
            scratch += [pltpu.VMEM(half, jnp.bfloat16), pltpu.VMEM(half, jnp.bfloat16)]
        scratch.append(pltpu.VMEM((ctx_count - 1,) + shard, jnp.bfloat16))
    return pl.pallas_call(
        partial(reduce_kernel, fsdp_count, ctx_count, chunk_count),
        out_shape=[jax.ShapeDtypeStruct(part.shape[2:], jnp.float32) for part in parts],
        in_specs=[pl.BlockSpec(memory_space=pltpu.VMEM)] * chunk_count,
        out_specs=[pl.BlockSpec(memory_space=pltpu.VMEM)] * chunk_count,
        scratch_shapes=scratch
        + [
            pltpu.SemaphoreType.DMA((chunk_count, slots)),
            pltpu.SemaphoreType.DMA((chunk_count, slots)),
        ],
        compiler_params=pltpu.CompilerParams(
            collective_id=1, has_side_effects=True, vmem_limit_bytes=VMEM_LIMIT
        ),
        name="reduce_grads",
    )(*parts)


def visible_pairs(seg_q_ref, seg_k_ref, place_ref):
    seg_q, seg_k = seg_q_ref[...], seg_k_ref[...]
    columns = lax.broadcasted_iota(jnp.int32, (seg_q.shape[0], seg_k.shape[1]), 1)
    return (seg_q == seg_k) & (place_ref[...] >= columns)


def attend_kernel(q_ref, k_ref, v_ref, seg_q_ref, seg_k_ref, place_ref, o_ref):
    visible = visible_pairs(seg_q_ref, seg_k_ref, place_ref)
    for head in range(q_ref.shape[0]):
        scores = times_transposed(q_ref[head], k_ref[...]) * HD ** (-0.5)
        scores = jnp.where(visible, scores, MASKED)
        exponent = jnp.exp(scores - jnp.max(scores, -1, keepdims=True))
        shares = exponent * (1.0 / jnp.sum(exponent, -1, keepdims=True))
        o_ref[head] = matmul(shares.astype(jnp.bfloat16), v_ref[...]).astype(jnp.bfloat16)


def attend_back_kernel(
    q_ref, k_ref, v_ref, go_ref, seg_q_ref, seg_k_ref, place_ref, gq_ref, gk_ref, gv_ref
):
    visible = visible_pairs(seg_q_ref, seg_k_ref, place_ref)
    key_total, value_total = None, None
    for head in range(q_ref.shape[0]):
        scores = times_transposed(q_ref[head], k_ref[...]) * HD ** (-0.5)
        scores = jnp.where(visible, scores, MASKED)
        exponent = jnp.exp(scores - jnp.max(scores, -1, keepdims=True))
        shares = exponent * (1.0 / jnp.sum(exponent, -1, keepdims=True))
        share_grad = times_transposed(go_ref[head], v_ref[...])
        row_dot = jnp.sum(shares * share_grad, -1, keepdims=True)
        score_grad = (shares * (share_grad - row_dot)).astype(jnp.bfloat16)
        gq_ref[head] = matmul(score_grad, k_ref[...]) * HD ** (-0.5)
        key_part = transposed_times(score_grad, q_ref[head])
        value_part = transposed_times(shares.astype(jnp.bfloat16), go_ref[head])
        key_total = key_part if key_total is None else key_total + key_part
        value_total = value_part if value_total is None else value_total + value_part
    gk_ref[...] = (key_total * HD ** (-0.5)).astype(jnp.bfloat16)
    gv_ref[...] = value_total.astype(jnp.bfloat16)


def attention_call(kernel, operands, masks, outs, name):
    micro_count, kv_count = operands[0].shape[:2]

    def spec(shape):
        rank = len(shape) - 2
        return pl.BlockSpec(
            (None, None) + tuple(shape[2:]), lambda micro, group: (micro, group) + (0,) * rank
        )

    seg_q, seg_k, place = masks
    return pl.pallas_call(
        kernel,
        grid=(micro_count, kv_count),
        out_shape=[jax.ShapeDtypeStruct(shape, kind) for shape, kind in outs],
        in_specs=[spec(operand.shape) for operand in operands]
        + [
            pl.BlockSpec((None,) + seg_q.shape[1:], lambda micro, group: (micro, 0, 0)),
            pl.BlockSpec((None,) + seg_k.shape[1:], lambda micro, group: (micro, 0, 0)),
            pl.BlockSpec(place.shape, lambda micro, group: (0, 0)),
        ],
        out_specs=[spec(shape) for shape, kind in outs],
        compiler_params=pltpu.CompilerParams(vmem_limit_bytes=VMEM_LIMIT),
        name=name,
    )(*operands, *masks)


def group_heads(values, micro_count):
    rows = values.reshape(micro_count, -1, KV, HEADS // KV, HD)
    return jnp.transpose(rows, (0, 2, 3, 1, 4))


def split_keys(pack_kv, micro_count):
    halves = pack_kv.reshape(micro_count, -1, 2, KV, HD)
    halves = jnp.transpose(halves, (2, 0, 3, 1, 4))
    return halves[0], halves[1]


def layer_forward(hidden_in, masks, local_pos, weights, micro_count):
    gain_pair, qkv_weight, out_weight, gate_up_weight, down_weight = weights
    row_count = hidden_in.shape[0]
    query_width = HEADS * HD
    kv_width = KV * HD
    hidden = hidden_in.astype(jnp.float32)
    normed = norm_scale(hidden, gain_pair[0]).astype(jnp.bfloat16)
    projected = matmul(normed, qkv_weight)
    queries = rotate(projected[:, :query_width].reshape(row_count, HEADS, HD), local_pos).astype(
        jnp.bfloat16
    )
    key_part = rotate(
        projected[:, query_width : query_width + kv_width].reshape(row_count, KV, HD), local_pos
    )
    local_kv = jnp.concatenate(
        [key_part.reshape(row_count, kv_width), projected[:, query_width + kv_width :]], -1
    ).astype(jnp.bfloat16)
    pack_kv = lax.all_gather(
        local_kv.reshape(micro_count, -1, 2 * kv_width), "ctx", axis=1, tiled=True
    )
    query_groups = group_heads(queries, micro_count)
    key_groups, value_groups = split_keys(pack_kv, micro_count)
    mixed_groups = attention_call(
        attend_kernel,
        (query_groups, key_groups, value_groups),
        masks,
        [(query_groups.shape, jnp.bfloat16)],
        "attend",
    )[0]
    mixed_low = jnp.transpose(mixed_groups, (0, 3, 1, 2, 4)).reshape(row_count, query_width)
    attended = hidden + matmul(mixed_low, out_weight)
    normed_two = norm_scale(attended, gain_pair[1]).astype(jnp.bfloat16)
    gate_up = matmul(normed_two, gate_up_weight)
    inner_rows = swiglu(gate_up).astype(jnp.bfloat16)
    result = (attended + matmul(inner_rows, down_weight)).astype(jnp.bfloat16)
    saved = (
        hidden,
        normed,
        (query_groups, key_groups, value_groups),
        mixed_low,
        attended,
        normed_two,
        gate_up,
        inner_rows,
    )
    return (result, saved)


def layer_backward(upstream, saved, masks, local_pos, weights, micro_count):
    gain_pair, qkv_weight, out_weight, gate_up_weight, down_weight = weights
    hidden, normed, groups, mixed_low, attended, normed_two, gate_up, inner_rows = saved
    row_count = hidden.shape[0]
    kv_width = KV * HD
    branch_grad = upstream.astype(jnp.bfloat16)
    inner_grad = times_transposed(branch_grad, down_weight)
    gate_up_grad = jax.vjp(swiglu, gate_up)[1](inner_grad)[0].astype(jnp.bfloat16)
    normed_two_grad = times_transposed(gate_up_grad, gate_up_weight)
    _, pull_two = jax.vjp(norm_scale, attended, gain_pair[1])
    attended_part, gain_two_grad = pull_two(normed_two_grad)
    attended_grad = upstream + attended_part
    out_branch = attended_grad.astype(jnp.bfloat16)
    mixed_grad = times_transposed(out_branch, out_weight).astype(jnp.bfloat16)
    query_groups, key_groups, value_groups = groups
    query_grad, key_grad, value_grad = attention_call(
        attend_back_kernel,
        (query_groups, key_groups, value_groups, group_heads(mixed_grad, micro_count)),
        masks,
        [
            (query_groups.shape, jnp.float32),
            (key_groups.shape, jnp.bfloat16),
            (value_groups.shape, jnp.bfloat16),
        ],
        "attend_back",
    )
    query_grad = jnp.transpose(query_grad, (0, 3, 1, 2, 4)).reshape(row_count, HEADS, HD)
    pack_kv_grad = jnp.transpose(jnp.stack([key_grad, value_grad]), (1, 3, 0, 2, 4))
    pack_kv_grad = pack_kv_grad.reshape(micro_count, -1, 2 * kv_width)
    local_kv_grad = (
        lax.psum_scatter(pack_kv_grad, "ctx", scatter_dimension=1, tiled=True)
        .astype(jnp.float32)
        .reshape(row_count, 2 * kv_width)
    )
    query_pre = rotate_back(query_grad, local_pos).reshape(row_count, HEADS * HD)
    key_pre = rotate_back(
        local_kv_grad[:, :kv_width].reshape(row_count, KV, HD), local_pos
    ).reshape(row_count, kv_width)
    projected_grad = jnp.concatenate([query_pre, key_pre, local_kv_grad[:, kv_width:]], -1).astype(
        jnp.bfloat16
    )
    normed_grad = times_transposed(projected_grad, qkv_weight)
    _, pull_one = jax.vjp(norm_scale, hidden, gain_pair[0])
    hidden_part, gain_one_grad = pull_one(normed_grad)
    input_grad = attended_grad + hidden_part

    def weight_grads():
        return (
            gain_one_grad,
            gain_two_grad,
            transposed_times(normed, projected_grad),
            transposed_times(mixed_low, out_branch),
            transposed_times(normed_two, gate_up_grad),
            transposed_times(inner_rows, branch_grad),
        )

    return (input_grad, weight_grads)


def on_device(tokens, cotangent, doc_lengths, norm_gains, w_qkv, w_out, w_gate_up, w_down):
    section_index = lax.axis_index("section")
    ctx_index = lax.axis_index("ctx")
    fsdp_count, ctx_count = lax.axis_size("fsdp"), lax.axis_size("ctx")
    micro_count, token_count, width = tokens.shape
    row_count = micro_count * token_count
    qkv_width = w_qkv.shape[2]
    half_ff = w_gate_up.shape[2] // 2
    spare = -(qkv_width + 2) % 128
    first_shard = jnp.concatenate(
        [w_qkv[0], norm_gains[0].T, jnp.zeros((w_qkv.shape[1], spare), jnp.bfloat16)], -1
    )
    shards = (
        first_shard,
        w_out[0],
        w_gate_up[0, :, :half_ff],
        w_gate_up[0, :, half_ff:],
        w_down[0],
    )
    fulls = gather_shards(shards, fsdp_count, ctx_count)
    fulls = [full.reshape(-1, full.shape[-1]) for full in fulls]
    gain_pair = fulls[0][:, qkv_width : qkv_width + 2].T.astype(jnp.float32)
    weights = (
        gain_pair,
        fulls[0][:, :qkv_width],
        fulls[1],
        jnp.concatenate([fulls[2], fulls[3]], -1),
        fulls[4],
    )
    offset = ctx_index * token_count
    seg_k, pos_k = jax.vmap(lambda lengths: layout(lengths, PACK))(doc_lengths[:, 0])
    seg_q = lax.dynamic_slice_in_dim(seg_k, offset, token_count, 1)
    local_pos = lax.dynamic_slice_in_dim(pos_k, offset, token_count, 1).reshape(row_count)
    place = offset + jnp.arange(token_count, dtype=jnp.int32)
    masks = (seg_q[:, :, None], seg_k[:, None, :], place[:, None])

    first_input = tokens.reshape(row_count, width)
    first_result, _ = layer_forward(first_input, masks, local_pos, weights, micro_count)
    incoming = shifted(first_result, "section", 1)
    hidden_in = jnp.where(section_index == 0, first_input, incoming)
    result, saved = layer_forward(hidden_in, masks, local_pos, weights, micro_count)
    given = cotangent.reshape(row_count, width).astype(jnp.float32)
    last_grad, _ = layer_backward(given, saved, masks, local_pos, weights, micro_count)
    incoming_grad = shifted(last_grad.astype(jnp.bfloat16), "section", -1)
    upstream = jnp.where(section_index == 1, given, incoming_grad.astype(jnp.float32))
    input_grad, weight_grads = layer_backward(
        upstream, saved, masks, local_pos, weights, micro_count
    )
    gain_one, gain_two, grad_qkv, grad_out, grad_gate_up, grad_down = weight_grads()
    spare_columns = jnp.zeros((width, spare), jnp.float32)
    first_grad = jnp.concatenate(
        [grad_qkv, gain_one[:, None], gain_two[:, None], spare_columns], -1
    )
    parts = (
        first_grad,
        grad_out,
        grad_gate_up[:, :half_ff],
        grad_gate_up[:, half_ff:],
        grad_down,
    )
    parts = [
        part.astype(jnp.bfloat16).reshape(fsdp_count, ctx_count, -1, part.shape[-1])
        for part in parts
    ]
    totals = reduce_parts(parts, fsdp_count, ctx_count)
    shape = (1, micro_count, token_count, width)
    return (
        result.reshape(shape),
        input_grad.reshape(shape),
        totals[0][None, :, qkv_width],
        totals[0][None, :, qkv_width + 1],
        totals[0][None, :, :qkv_width],
        totals[1][None],
        jnp.concatenate([totals[2], totals[3]], -1)[None],
        totals[4][None],
    )


def solution(mesh):
    return jax.shard_map(
        on_device,
        mesh=mesh,
        in_specs=(
            P(None, ("fsdp", "ctx"), None),
            P(None, ("fsdp", "ctx"), None),
            P(None, "fsdp", None),
            P("section", None, ("fsdp", "ctx")),
            P("section", ("fsdp", "ctx"), None),
            P("section", ("fsdp", "ctx"), None),
            P("section", ("fsdp", "ctx"), None),
            P("section", ("fsdp", "ctx"), None),
        ),
        out_specs=(
            P("section", None, ("fsdp", "ctx"), None),
            P("section", None, ("fsdp", "ctx"), None),
            P("section", ("fsdp", "ctx")),
            P("section", ("fsdp", "ctx")),
            P("section", ("fsdp", "ctx"), None),
            P("section", ("fsdp", "ctx"), None),
            P("section", ("fsdp", "ctx"), None),
            P("section", ("fsdp", "ctx"), None),
        ),
        check_vma=False,
    )
```

time: 826 us -> 554 us (0.67)
  Pallas kernels: 0 us -> 216 us
  waiting for transfers between devices: 320 us -> 112 us
  blocking collectives: 193 us -> 0 us
  matrix products: 134 us -> 50.8 us
  local copies, waits for them, and re-layouts: 91.2 us -> 117 us
  other arithmetic: 47.1 us -> 31.2 us
    unnamed x8 -> x4, waiting for transfers between devices: 225 us -> 0.07 us
    pallas_call x0 -> x6, Pallas kernels: none -> 216 us  [the longest x4 79.4 us: attention_call(): pl.pallas_call(kernel, grid=(micro_count, kv_count), out_shape=[jax.Shape...]
    all_gather x5 -> x0, blocking collectives: 157 us -> none  [the longest x1 62.8 us: on_device(): lax.all_gather(shards[2], ('fsdp', 'ctx'), axis=1, tiled=True)]
    dot_general x42 -> x0, matrix products: 58.3 us -> none  [the longest x6 12.9 us: group_forward(): jnp.einsum('gqp,pd->qgd', shares, value_group, preferred_element_type=jnp...]
    all_gather x3 -> x2, waiting for transfers between devices: 7 us -> 59.3 us  [layer_forward(): lax.all_gather(local_kv.reshape(micro_count, -1, 2 * kv_width), 'ctx', ax...]
    reshape x0 -> x19, local copies, waits for them, and re-layouts: none -> 47.7 us  [the longest x4 9.69 us: group_heads(): rows = values.reshape(micro_count, -1, KV, HEADS // KV, HD)]
    reduce_scatter x3 -> x2, waiting for transfers between devices: 69.7 us -> 24.3 us  [layer_backward(): lax.psum_scatter(pack_kv_grad, 'ctx', scatter_dimension=1, tiled=True)]
    unnamed x1 -> x0, blocking collectives: 36 us -> none
  transfers between devices with their start and end apart: 11 -> 6, of which waited for: 8 -> 5; matrix products, arithmetic and copies ran while one was open for 14% -> 13% of each run, Pallas kernels for 0% -> 0%
where the time goes in v1:
time: 554 us; the launch traced here: 548 us
  Pallas kernels  216 us (39%)
  local copies, waits for them, and re-layouts  117 us (21%)
  waiting for transfers between devices  112 us (20%)
  matrix products  50.8 us (9%)
  other arithmetic  31.2 us (6%)
  between operations  14.9 us (3%)
    pallas_call x4, Pallas kernels, attention_call(): pl.pallas_call(kernel, grid=(micro_count, kv_count), out_shape=[jax.Shape...  79.4 us
    pallas_call x1, Pallas kernels, reduce_parts(): pl.pallas_call(partial(reduce_kernel, fsdp_count, ctx_count, chunk_count)...  69.8 us
    pallas_call x1, Pallas kernels, gather_shards(): pl.pallas_call(partial(gather_kernel, fsdp_count, ctx_count, chunk_count)...  66.8 us
    all_gather x2, waiting for transfers between devices, layer_forward(): lax.all_gather(local_kv.reshape(micro_count, -1, 2 * kv_width), 'ctx', ax...  59.3 us
    ppermute x2, waiting for transfers between devices, shifted(): lax.ppermute(value, axis, [(source, source + steps) for source in range(l...  28.4 us
    reduce_scatter x2, waiting for transfers between devices, layer_backward(): lax.psum_scatter(pack_kv_grad, 'ctx', scatter_dimension=1, tiled=True)  24.3 us
    dot_general x8, matrix products, times_transposed(): lax.dot_general(left_side, right_side, (((1,), (1,)), ((), ())), preferre...  21.9 us
    dot_general x8, matrix products, matmul(): return jnp.dot(left_side, right_side, preferred_element_type=jnp.float32)  16.9 us
  transfers between devices with their start and end apart: 6, of which 5 were waited for; matrix products, arithmetic and copies ran while one was open for 13% of the time, Pallas kernels for 0%

profile of v1, /device:TPU:0, one launch (start us, length us, event | category | flops | bytes accessed | tf_op | source)
XLA Modules:
  0.0 547.6 jit_solution(6729791378870541484)
XLA Ops:
  11.8 66.8 %gather_weights.1 = (bf16[4,4,36,1024]{3,2,1,0:T(8,128)(2,1)}, bf16[4,4,36,576]{3,2,1,0:T(8,128)(2,1)}, bf16[4,4,36,1536]{3,2,1,0:T(8,128)(2,1)}, bf16[4,4,36,15...) custom-call(bf16[36,1024]{1,0:T(8,128)(2,1)} %maximum_maximum_fusion.1.refs_0_, bf16[36,576]{1,0:T(8,128)(2,1)} %bitcast.197, ...), custom_call_target="tpu_custom_call" | custom-call | tf_op jit(solution)/shard_map/gather_weights/pallas_call | solution.py:184
  100.7 28.4 %all-gather.3.cloned.1.call-done = bf16[2,1024,384]{1,0,2:T(2,128)(2,1)} async-done(((bf16[2,256,384]{1,0,2:T(2,128)(2,1)}), bf16[2,1024,384]{1,0,2:T(2,128)(2,1)}) %all-gather.3.cloned.1.call-update) | async-done | bytes 1572880 | tf_op jit(solution)/shard_map/all_gather | solution.py:406
  129.1 5.5 copy.187
  134.6 3.8 slice_bitcast_fusion.2
  138.4 15.6 %attend.2 = bf16[2,3,3,256,64]{4,3,2,1,0:T(8,128)(2,1)} custom-call(bf16[2,3,3,256,64]{4,3,2,1,0:T(8,128)(2,1)} %maximum_bitcast_fusion.2.q_ref, bf16[2,3,1024,64]{3,2,1,0:T(8,128)(2,1)} %get-tuple-element.108.k_ref, bf16[2,3,1024,64]{3,2,1,0:T(8,128)(2,1)} %get-tuple-element.107.v_ref, s32[2,256,1]{2,1,0:T(8,128)} %copy.188.seg_q_ref, ...), custom_call_target="tpu_custom_call" | custom-call | tf_op jit(solution)/shard_map/attend/pallas_call | solution.py:362
  168.1 12.7 %collective-permute-done = bf16[512,576]{0,1:T(8,128)(2,1)S(1)} collective-permute-done((bf16[512,576]{0,1:T(8,128)(2,1)S(1)}, bf16[512,576]{0,1:T(8,128)(2,1)S(1)}, u32[]{:S(2)}, u32[]{:S(2)}) %collective-permute-start) | collective-permute-done | bytes 589856 | tf_op jit(solution)/shard_map/ppermute | solution.py:24
  190.6 30.9 %all-gather.5.cloned.1.call-done = bf16[2,1024,384]{1,0,2:T(2,128)(2,1)} async-done(((bf16[2,256,384]{1,0,2:T(2,128)(2,1)}), bf16[2,1024,384]{1,0,2:T(2,128)(2,1)}) %all-gather.5.cloned.1.call-update) | async-done | bytes 1572880 | tf_op jit(solution)/shard_map/all_gather | solution.py:406
  221.5 4.2 copy.193
  227.5 15.6 %attend.3 = bf16[2,3,3,256,64]{4,3,2,1,0:T(8,128)(2,1)} custom-call(bf16[2,3,3,256,64]{4,3,2,1,0:T(8,128)(2,1)} %maximum_bitcast_fusion.3.q_ref, bf16[2,3,1024,64]{3,2,1,0:T(8,128)(2,1)} %get-tuple-element.106.k_ref, bf16[2,3,1024,64]{3,2,1,0:T(8,128)(2,1)} %get-tuple-element.105.v_ref, s32[2,256,1]{2,1,0:T(8,128)} %copy.188.seg_q_ref, ...), custom_call_target="tpu_custom_call" | custom-call | tf_op jit(solution)/shard_map/attend/pallas_call | solution.py:362
  263.9 24.3 %attend_back.2 = (f32[2,3,3,256,64]{4,3,2,1,0:T(8,128)}, bf16[2,3,1024,64]{3,2,1,0:T(8,128)(2,1)}, bf16[2,3,1024,64]{3,2,1,0:T(8,128)(2,1)}) custom-call(bf16[2,3,3,256,64]{4,3,2,1,0:T(8,128)(2,1)} %maximum_bitcast_fusion.3.q_ref, bf16[2,3,1024,64]{3,2,1,0:T(8,128)(2,1)} %get-tuple-element.106.k_ref, bf16[2,3,1024,64]{3,2,1,0:T(8,128)(2,1)} %get-tuple-element.105.v_ref, ...), custom_call_target="tpu_custom_call" | custom-call | tf_op jit(solution)/shard_map/attend_back/pallas_call | solution.py:362
  288.2 4.3 maximum_bitcast_fusion
  292.5 4.3 copy.201
  296.9 3.8 copy.200
  306.3 24.3 %reduce-scatter.3.cloned.1.call-done = bf16[2,256,384]{1,2,0:T(8,128)(2,1)} async-done(((bf16[2,1024,384]{1,2,0:T(8,128)(2,1)}), bf16[2,256,384]{1,2,0:T(8,128)(2,1)}) %reduce-scatter.3.cloned.1.call-update) | async-done | bytes 393232 | tf_op jit(solution)/shard_map/reduce_scatter | solution.py:467
  344.8 15.7 %collective-permute-done.1 = bf16[512,576]{0,1:T(8,128)(2,1)S(1)} collective-permute-done((bf16[512,576]{0,1:T(8,128)(2,1)}, bf16[512,576]{0,1:T(8,128)(2,1)S(1)}, u32[]{:S(2)}, u32[]{:S(2)}) %collective-permute-start.1) | collective-permute-done | bytes 589856 | tf_op jit(solution)/shard_map/ppermute | solution.py:24
  360.4 6.1 %fusion.69 = (f32[512,1536]{1,0:T(8,128)S(1)}, f32[512,1536]{1,0:T(8,128)S(1)}, bf16[512,1536]{1,0:T(8,128)(2,1)}) fusion(f32[512,3072]{1,0:T(8,128)} %copy-done.13, bf16[1536,576]{1,0:T(8,128)(2,1)} %bitcast.207, bf16[512,576]{0,1:T(8,128)(2,1)S(1)} %collective-permute-done.1, bf16[512,576]{0,1:T(8,128)(2,1)S(1)} %bitcast.151, pred[]{:T(512)S(6)} %eq.23), kind=kOutput, calls=%fused_computation.167 | convolution fusion | flops 918159360 | bytes 17104896 | tf_op jit(solution)/shard_map/dot_general | solution.py:32
  374.9 23.8 %attend_back.3 = (f32[2,3,3,256,64]{4,3,2,1,0:T(8,128)}, bf16[2,3,1024,64]{3,2,1,0:T(8,128)(2,1)}, bf16[2,3,1024,64]{3,2,1,0:T(8,128)(2,1)}) custom-call(bf16[2,3,3,256,64]{4,3,2,1,0:T(8,128)(2,1)} %maximum_bitcast_fusion.3.q_ref, bf16[2,3,1024,64]{3,2,1,0:T(8,128)(2,1)} %get-tuple-element.106.k_ref, bf16[2,3,1024,64]{3,2,1,0:T(8,128)(2,1)} %get-tuple-element.105.v_ref, ...), custom_call_target="tpu_custom_call" | custom-call | tf_op jit(solution)/shard_map/attend_back/pallas_call | solution.py:362
  398.7 4.3 maximum_bitcast_fusion.1
  403.0 4.3 copy.208
  407.4 4.0 fusion.11
  420.2 4.9 convolution_convert_fusion
  434.6 3.9 copy.214
  438.5 3.9 copy.207
  460.5 69.8 %reduce_grads.1 = (f32[36,1024]{1,0:T(8,128)}, f32[36,576]{1,0:T(8,128)}, f32[36,1536]{1,0:T(8,128)}, f32[36,1536]{1,0:T(8,128)}, f32[96,576]{1,0:T(8,128)}) custom-call(bf16[4,4,36,1024]{3,2,1,0:T(8,128)(2,1)} %maximum_maximum_fusion.refs_0_, bf16[4,4,36,576]{3,2,1,0:T(8,128)(2,1)} %reshape.345.refs_1_, bf16[4,4,36,1536]{3,2,1,0:T(8,128)(2,1)} %reshape.346.refs_2_, ...), custom_call_target="tpu_custom_call" | custom-call | tf_op jit(solution)/shard_map/reduce_grads/pallas_call | solution.py:297
  (245 shorter events, 147.4 us)
Async XLA Ops:
  7.2 3.8 copy-start.25
  7.2 3.9 copy-start.39
  7.2 122.0 %all-gather.3.cloned.1.call-start = ((), (), s32[]{:S(2)}) async-start(), calls=%async_computation.2 | async-start | bytes 1966080 | tf_op jit(solution)/shard_map/all_gather | solution.py:406
  11.0 70.1 %copy-start.14 = (bf16[2,72,8,256]{3,2,0,1:T(8,128)(2,1)}, bf16[2,72,8,256]{3,2,0,1:T(8,128)(2,1)S(1)}, u32[]{:S(2)}) copy-start(bf16[2,72,8,256]{3,2,0,1:T(8,128)(2,1)S(1)} %copy.227) | copy-start | bytes 1769476
  84.4 9.8 %copy-start.18 = (f32[512,32]{0,1:T(8,128)}, f32[512,32]{0,1:T(8,128)S(1)}, u32[]{:S(2)}) copy-start(f32[512,32]{0,1:T(8,128)S(1)} %get-tuple-element.131) | copy-start | bytes 196612
  84.4 9.8 %copy-start.20 = (f32[512,32]{0,1:T(8,128)}, f32[512,32]{0,1:T(8,128)S(1)}, u32[]{:S(2)}) copy-start(f32[512,32]{0,1:T(8,128)S(1)} %get-tuple-element.132) | copy-start | bytes 196612
  85.8 135.6 %all-gather.5.cloned.1.call-start = ((), (), s32[]{:S(2)}) async-start(), calls=%async_computation.3 | async-start | bytes 1966080 | tf_op jit(solution)/shard_map/all_gather | solution.py:406
  89.1 3.7 copy-start.26
  100.7 59.5 %copy-start = (bf16[576,3072]{1,0:T(8,128)(2,1)}, bf16[576,3072]{1,0:T(8,128)(2,1)S(1)}, u32[]{:S(2)}) copy-start(bf16[576,3072]{1,0:T(8,128)(2,1)S(1)} %constant_dynamic-update-slice_fusion) | copy-start | bytes 10616836
  163.0 17.8 %copy-start.15 = (bf16[2,72,8,256]{3,2,0,1:T(8,128)(2,1)S(1)}, bf16[2,72,8,256]{3,2,0,1:T(8,128)(2,1)}, u32[]{:S(2)}) copy-start(bf16[2,72,8,256]{3,2,0,1:T(8,128)(2,1)} %copy-done.14) | copy-start | bytes 1769476
  164.4 16.6 %copy-start.28 = (bf16[576,1024]{1,0:T(8,128)(2,1)S(1)}, bf16[576,1024]{1,0:T(8,128)(2,1)}, u32[]{:S(2)}) copy-start(bf16[576,1024]{1,0:T(8,128)(2,1)} %copy-done.27) | copy-start | bytes 3538948
  164.5 16.6 %copy-start.41 = (f32[576]{0:T(1024)S(1)}, f32[576]{0:T(1024)}, u32[]{:S(2)}) copy-start(f32[576]{0:T(1024)} %copy-done.40) | copy-start | bytes 6916
  164.5 16.3 %collective-permute-start = (bf16[512,576]{0,1:T(8,128)(2,1)S(1)}, bf16[512,576]{0,1:T(8,128)(2,1)S(1)}, u32[]{:S(2)}, u32[]{:S(2)}) collective-permute-start(bf16[512,576]{0,1:T(8,128)(2,1)S(1)} %fusion.12), channel_id=1, source_target_pairs={{0,16},{1,17},{2,18},{3,19},{4,20},{5,21},{6,22},{7,23},{8,24},{9,... | collective-permute-start | bytes 1769480 | tf_op jit(solution)/shard_map/ppermute | solution.py:24
  184.4 146.1 %reduce-scatter.3.cloned.1.call-start = ((), (), s32[]{:S(2)}) async-start(), calls=%async_computation.4 | async-start | bytes 1966080 | tf_op jit(solution)/shard_map/reduce_scatter | solution.py:467
  296.9 152.6 %reduce-scatter.5.cloned.1.call-start = ((), (), s32[]{:S(2)}) async-start(), calls=%async_computation.5 | async-start | bytes 1966080 | tf_op jit(solution)/shard_map/reduce_scatter | solution.py:467
  336.0 3.6 copy-start.42
  343.5 17.0 %collective-permute-start.1 = (bf16[512,576]{0,1:T(8,128)(2,1)}, bf16[512,576]{0,1:T(8,128)(2,1)S(1)}, u32[]{:S(2)}, u32[]{:S(2)}) collective-permute-start(bf16[512,576]{0,1:T(8,128)(2,1)} %fusion.20), channel_id=1, source_target_pairs={{16,0},{17,1},{18,2},{19,3},{20,4},{21,5},{22,6},{23,7},{24,8},{25... | collective-permute-start | bytes 1769480 | tf_op jit(solution)/shard_map/ppermute | solution.py:24
  344.8 21.8 %copy-start.2 = (bf16[576,3072]{1,0:T(8,128)(2,1)S(1)}, bf16[576,3072]{1,0:T(8,128)(2,1)}, u32[]{:S(2)}) copy-start(bf16[576,3072]{1,0:T(8,128)(2,1)} %copy-done) | copy-start | bytes 10616836
  360.4 6.1 %copy-start.31 = (bf16[512,576]{0,1:T(8,128)(2,1)}, bf16[512,576]{0,1:T(8,128)(2,1)S(1)}, u32[]{:S(2)}) copy-start(bf16[512,576]{0,1:T(8,128)(2,1)S(1)} %collective-permute-done.1) | copy-start | bytes 1769476
  411.3 4.9 copy-start.17
  427.3 3.6 copy-start.6
  427.3 3.6 copy-start.33
  460.5 72.3 %copy-start.29 = (f32[512,576]{0,1:T(8,128)S(1)}, f32[512,576]{0,1:T(8,128)}, u32[]{:S(2)}) copy-start(f32[512,576]{0,1:T(8,128)} %get-tuple-element.142) | copy-start | bytes 3538948
  460.5 72.3 %copy-start.43 = (f32[576]{0:T(1024)S(1)}, f32[576]{0:T(1024)}, u32[]{:S(2)}) copy-start(f32[576]{0:T(1024)} %copy-done.40) | copy-start | bytes 6916
  (32 other events, 68.5 us)
Sparse Core Ops, SparseCore 0:
  86.0 43.1 all-gather.2
  184.6 36.8 all-gather.4
  297.0 33.5 reduce-scatter.2
  407.5 33.5 reduce-scatter.4

commit v2 on v1

--- a/solution.py
+++ b/solution.py
@@ -47,28 +47,6 @@
 def swiglu(gate_up):
     half_width = gate_up.shape[1] // 2
     return jax.nn.silu(gate_up[:, :half_width]) * gate_up[:, half_width:]
-
-
-def rotate(values, docpos):
-    half_size = values.shape[-1] // 2
-    frequency = ROPE_BASE ** (-(jnp.arange(half_size, dtype=jnp.float32) * 2.0 / values.shape[-1]))
-    angles = docpos[:, None] * frequency[None, :]
-    cosine = jnp.cos(angles)[:, None, :]
-    sine_rows = jnp.sin(angles)[:, None, :]
-    lower_half = values[..., :half_size]
-    upper_half = values[..., half_size:]
-    return jnp.concatenate(
-        [
-            lower_half * cosine - upper_half * sine_rows,
-            upper_half * cosine + lower_half * sine_rows,
-        ],
-        -1,
-    )
-
-
-def rotate_back(grads, docpos):
-    _, pullback = jax.vjp(partial(rotate, docpos=docpos), jnp.zeros(grads.shape, jnp.float32))
-    return pullback(grads)[0]
 
 
 def layout(lengths, pack_len):
@@ -159,10 +137,13 @@
     for copy in own:
         copy.start()
     meet(fsdp_me, ctx_me, fsdp_count, ctx_count)
+    for chunk in range(chunk_count):
+        for copy in copies(chunk, 0):
+            copy.start()
     for turn in range(chunk_count + stage_count):
         for chunk in range(chunk_count):
             stage = turn - chunk
-            if stage < 0 or stage > stage_count:
+            if stage < 1 or stage > stage_count:
                 continue
             if stage == 1:
                 own[chunk].wait()
@@ -266,15 +247,17 @@
             lax.fori_loop(0, ctx_count, add, 0)
 
     meet(fsdp_me, ctx_me, fsdp_count, ctx_count)
+    for chunk in range(chunk_count):
+        for copy in copies(chunk, 0):
+            copy.start()
     for turn in range(chunk_count + level_count + 1):
         for chunk in range(chunk_count):
             stage = turn - chunk
-            if stage < 0 or stage > level_count + 1:
+            if stage < 1 or stage > level_count + 1:
                 continue
-            if stage >= 1:
-                for copy in copies(chunk, stage - 1):
-                    copy.wait_recv()
-                absorb(chunk, stage - 1)
+            for copy in copies(chunk, stage - 1):
+                copy.wait_recv()
+            absorb(chunk, stage - 1)
             if stage <= level_count:
                 for copy in copies(chunk, stage):
                     copy.start()
@@ -317,105 +300,143 @@
     return (seg_q == seg_k) & (place_ref[...] >= columns)
 
 
-def attend_kernel(q_ref, k_ref, v_ref, seg_q_ref, seg_k_ref, place_ref, o_ref):
+def turned(values, cosine, signed_sine):
+    lanes = lax.broadcasted_iota(jnp.int32, values.shape, 1)
+    half = HD // 2
+    other = jnp.where(
+        lanes % HD < half,
+        pltpu.roll(values, values.shape[1] - half, 1),
+        pltpu.roll(values, half, 1),
+    )
+    return values * cosine + other * signed_sine
+
+
+def project_kernel(h_ref, gain_ref, w_ref, cos_ref, sin_ref, normed_ref, q_ref, kv_ref, row_ref):
+    hidden = h_ref[...].astype(jnp.float32)
+    normed = norm_scale(hidden, gain_ref[...]).astype(jnp.bfloat16)
+    normed_ref[...] = normed
+    turned_width = (HEADS + KV) * HD
+    for first in range(0, w_ref.shape[1], 128):
+        block = matmul(normed, w_ref[:, first : first + 128])
+        if first < turned_width:
+            block = turned(block, cos_ref[...], sin_ref[...])
+        row_ref[:, first : first + 128] = block
+    q_ref[...] = (row_ref[:, : HEADS * HD] * HD ** (-0.5)).astype(jnp.bfloat16)
+    kv_ref[...] = row_ref[:, HEADS * HD : (HEADS + 2 * KV) * HD].astype(jnp.bfloat16)
+
+
+def project(hidden_in, gain, weight, cosine, signed_sine):
+    rows, width = hidden_in.shape
+    return pl.pallas_call(
+        project_kernel,
+        out_shape=[
+            jax.ShapeDtypeStruct((rows, width), jnp.bfloat16),
+            jax.ShapeDtypeStruct((rows, HEADS * HD), jnp.bfloat16),
+            jax.ShapeDtypeStruct((rows, 2 * KV * HD), jnp.bfloat16),
+        ],
+        scratch_shapes=[pltpu.VMEM((rows, weight.shape[1]), jnp.float32)],
+        compiler_params=pltpu.CompilerParams(vmem_limit_bytes=VMEM_LIMIT),
+        name="project",
+    )(hidden_in, gain, weight, cosine, signed_sine)
+
+
+def unturn_kernel(gq_ref, gkv_ref, cos_ref, sin_ref, out_ref, row_ref):
+    query_width = HEADS * HD
+    row_ref[:, :query_width] = gq_ref[...] * HD ** (-0.5)
+    row_ref[:, query_width : query_width + 2 * KV * HD] = gkv_ref[...].astype(jnp.float32)
+    for first in range(0, (HEADS + KV) * HD, 128):
+        block = row_ref[:, first : first + 128]
+        row_ref[:, first : first + 128] = turned(block, cos_ref[...], -sin_ref[...])
+    out_ref[...] = row_ref[...].astype(jnp.bfloat16)
+
+
+def unturn(query_grad, kv_grad, cosine, signed_sine):
+    rows = query_grad.shape[0]
+    width = (HEADS + 2 * KV) * HD
+    return pl.pallas_call(
+        unturn_kernel,
+        out_shape=jax.ShapeDtypeStruct((rows, width), jnp.bfloat16),
+        scratch_shapes=[pltpu.VMEM((rows, width), jnp.float32)],
+        compiler_params=pltpu.CompilerParams(vmem_limit_bytes=VMEM_LIMIT),
+        name="unturn",
+    )(query_grad, kv_grad, cosine, signed_sine)
+
+
+def columns_of(head):
+    return slice(head * HD, (head + 1) * HD)
+
+
+def attend_kernel(q_ref, kv_ref, seg_q_ref, seg_k_ref, place_ref, o_ref, log_ref):
     visible = visible_pairs(seg_q_ref, seg_k_ref, place_ref)
-    for head in range(q_ref.shape[0]):
-        scores = times_transposed(q_ref[head], k_ref[...]) * HD ** (-0.5)
+    for head in range(HEADS):
+        group = head // (HEADS // KV)
+        scores = times_transposed(q_ref[:, columns_of(head)], kv_ref[:, columns_of(group)])
         scores = jnp.where(visible, scores, MASKED)
-        exponent = jnp.exp(scores - jnp.max(scores, -1, keepdims=True))
-        shares = exponent * (1.0 / jnp.sum(exponent, -1, keepdims=True))
-        o_ref[head] = matmul(shares.astype(jnp.bfloat16), v_ref[...]).astype(jnp.bfloat16)
+        row_max = jnp.max(scores, -1, keepdims=True)
+        exponent = jnp.exp(scores - row_max)
+        row_sum = jnp.sum(exponent, -1, keepdims=True)
+        mixed = matmul(exponent.astype(jnp.bfloat16), kv_ref[:, columns_of(KV + group)])
+        o_ref[:, columns_of(head)] = (mixed * (1.0 / row_sum)).astype(jnp.bfloat16)
+        log_ref[:, head : head + 1] = row_max + jnp.log(row_sum)
 
 
 def attend_back_kernel(
-    q_ref, k_ref, v_ref, go_ref, seg_q_ref, seg_k_ref, place_ref, gq_ref, gk_ref, gv_ref
+    q_ref, kv_ref, go_ref, log_ref, seg_q_ref, seg_k_ref, place_ref, gq_ref, gkv_ref
 ):
     visible = visible_pairs(seg_q_ref, seg_k_ref, place_ref)
-    key_total, value_total = None, None
-    for head in range(q_ref.shape[0]):
-        scores = times_transposed(q_ref[head], k_ref[...]) * HD ** (-0.5)
-        scores = jnp.where(visible, scores, MASKED)
-        exponent = jnp.exp(scores - jnp.max(scores, -1, keepdims=True))
-        shares = exponent * (1.0 / jnp.sum(exponent, -1, keepdims=True))
-        share_grad = times_transposed(go_ref[head], v_ref[...])
-        row_dot = jnp.sum(shares * share_grad, -1, keepdims=True)
-        score_grad = (shares * (share_grad - row_dot)).astype(jnp.bfloat16)
-        gq_ref[head] = matmul(score_grad, k_ref[...]) * HD ** (-0.5)
-        key_part = transposed_times(score_grad, q_ref[head])
-        value_part = transposed_times(shares.astype(jnp.bfloat16), go_ref[head])
-        key_total = key_part if key_total is None else key_total + key_part
-        value_total = value_part if value_total is None else value_total + value_part
-    gk_ref[...] = (key_total * HD ** (-0.5)).astype(jnp.bfloat16)
-    gv_ref[...] = value_total.astype(jnp.bfloat16)
-
-
-def attention_call(kernel, operands, masks, outs, name):
-    micro_count, kv_count = operands[0].shape[:2]
-
-    def spec(shape):
-        rank = len(shape) - 2
-        return pl.BlockSpec(
-            (None, None) + tuple(shape[2:]), lambda micro, group: (micro, group) + (0,) * rank
-        )
-
-    seg_q, seg_k, place = masks
+    for group in range(KV):
+        key_total, value_total = None, None
+        for head in range(group * (HEADS // KV), (group + 1) * (HEADS // KV)):
+            query = q_ref[:, columns_of(head)]
+            grad = go_ref[:, columns_of(head)]
+            keys = kv_ref[:, columns_of(group)]
+            scores = times_transposed(query, keys)
+            scores = jnp.where(visible, scores - log_ref[:, head : head + 1], MASKED)
+            shares = jnp.exp(scores)
+            share_grad = times_transposed(grad, kv_ref[:, columns_of(KV + group)])
+            row_dot = jnp.sum(shares * share_grad, -1, keepdims=True)
+            score_grad = (shares * (share_grad - row_dot)).astype(jnp.bfloat16)
+            gq_ref[:, columns_of(head)] = matmul(score_grad, keys)
+            key_part = transposed_times(score_grad, query)
+            value_part = transposed_times(shares.astype(jnp.bfloat16), grad)
+            key_total = key_part if key_total is None else key_total + key_part
+            value_total = value_part if value_total is None else value_total + value_part
+        gkv_ref[:, columns_of(group)] = key_total.astype(jnp.bfloat16)
+        gkv_ref[:, columns_of(KV + group)] = value_total.astype(jnp.bfloat16)
+
+
+def local_call(kernel, operands, outs, name):
     return pl.pallas_call(
         kernel,
-        grid=(micro_count, kv_count),
         out_shape=[jax.ShapeDtypeStruct(shape, kind) for shape, kind in outs],
-        in_specs=[spec(operand.shape) for operand in operands]
-        + [
-            pl.BlockSpec((None,) + seg_q.shape[1:], lambda micro, group: (micro, 0, 0)),
-            pl.BlockSpec((None,) + seg_k.shape[1:], lambda micro, group: (micro, 0, 0)),
-            pl.BlockSpec(place.shape, lambda micro, group: (0, 0)),
-        ],
-        out_specs=[spec(shape) for shape, kind in outs],
         compiler_params=pltpu.CompilerParams(vmem_limit_bytes=VMEM_LIMIT),
+        cost_estimate=pl.CostEstimate(
+            flops=4_000_000_000, bytes_accessed=8_000_000, transcendentals=3_000_000
+        ),
         name=name,
-    )(*operands, *masks)
-
-
-def group_heads(values, micro_count):
-    rows = values.reshape(micro_count, -1, KV, HEADS // KV, HD)
-    return jnp.transpose(rows, (0, 2, 3, 1, 4))
-
-
-def split_keys(pack_kv, micro_count):
-    halves = pack_kv.reshape(micro_count, -1, 2, KV, HD)
-    halves = jnp.transpose(halves, (2, 0, 3, 1, 4))
-    return halves[0], halves[1]
-
-
-def layer_forward(hidden_in, masks, local_pos, weights, micro_count):
+    )(*operands)
+
+
+def layer_forward(hidden_in, masks, turns, weights, micro_count):
     gain_pair, qkv_weight, out_weight, gate_up_weight, down_weight = weights
-    row_count = hidden_in.shape[0]
-    query_width = HEADS * HD
-    kv_width = KV * HD
     hidden = hidden_in.astype(jnp.float32)
-    normed = norm_scale(hidden, gain_pair[0]).astype(jnp.bfloat16)
-    projected = matmul(normed, qkv_weight)
-    queries = rotate(projected[:, :query_width].reshape(row_count, HEADS, HD), local_pos).astype(
-        jnp.bfloat16
-    )
-    key_part = rotate(
-        projected[:, query_width : query_width + kv_width].reshape(row_count, KV, HD), local_pos
-    )
-    local_kv = jnp.concatenate(
-        [key_part.reshape(row_count, kv_width), projected[:, query_width + kv_width :]], -1
-    ).astype(jnp.bfloat16)
-    pack_kv = lax.all_gather(
-        local_kv.reshape(micro_count, -1, 2 * kv_width), "ctx", axis=1, tiled=True
-    )
-    query_groups = group_heads(queries, micro_count)
-    key_groups, value_groups = split_keys(pack_kv, micro_count)
-    mixed_groups = attention_call(
-        attend_kernel,
-        (query_groups, key_groups, value_groups),
-        masks,
-        [(query_groups.shape, jnp.bfloat16)],
-        "attend",
-    )[0]
-    mixed_low = jnp.transpose(mixed_groups, (0, 3, 1, 2, 4)).reshape(row_count, query_width)
+    normed, queries, local_kv = project(hidden_in, gain_pair[:1], qkv_weight, *turns)
+    count = hidden.shape[0] // micro_count
+    packs, mixed_parts, log_parts = [], [], []
+    for micro in range(micro_count):
+        rows = slice(micro * count, (micro + 1) * count)
+        packs.append(lax.all_gather(local_kv[rows], "ctx", axis=0, tiled=True))
+    for micro in range(micro_count):
+        rows = slice(micro * count, (micro + 1) * count)
+        mixed, logs = local_call(
+            attend_kernel,
+            (queries[rows], packs[micro]) + masks[micro],
+            [((count, HEADS * HD), jnp.bfloat16), ((count, HEADS), jnp.float32)],
+            "attend",
+        )
+        mixed_parts.append(mixed)
+        log_parts.append(logs)
+    mixed_low = jnp.concatenate(mixed_parts, 0)
     attended = hidden + matmul(mixed_low, out_weight)
     normed_two = norm_scale(attended, gain_pair[1]).astype(jnp.bfloat16)
     gate_up = matmul(normed_two, gate_up_weight)
@@ -424,7 +445,7 @@
     saved = (
         hidden,
         normed,
-        (query_groups, key_groups, value_groups),
+        (queries, packs, log_parts),
         mixed_low,
         attended,
         normed_two,
@@ -434,11 +455,10 @@
     return (result, saved)
 
 
-def layer_backward(upstream, saved, masks, local_pos, weights, micro_count):
+def layer_backward(upstream, saved, masks, turns, weights, micro_count):
     gain_pair, qkv_weight, out_weight, gate_up_weight, down_weight = weights
-    hidden, normed, groups, mixed_low, attended, normed_two, gate_up, inner_rows = saved
-    row_count = hidden.shape[0]
-    kv_width = KV * HD
+    hidden, normed, parts, mixed_low, attended, normed_two, gate_up, inner_rows = saved
+    count = hidden.shape[0] // micro_count
     branch_grad = upstream.astype(jnp.bfloat16)
     inner_grad = times_transposed(branch_grad, down_weight)
     gate_up_grad = jax.vjp(swiglu, gate_up)[1](inner_grad)[0].astype(jnp.bfloat16)
@@ -448,34 +468,22 @@
     attended_grad = upstream + attended_part
     out_branch = attended_grad.astype(jnp.bfloat16)
     mixed_grad = times_transposed(out_branch, out_weight).astype(jnp.bfloat16)
-    query_groups, key_groups, value_groups = groups
-    query_grad, key_grad, value_grad = attention_call(
-        attend_back_kernel,
-        (query_groups, key_groups, value_groups, group_heads(mixed_grad, micro_count)),
-        masks,
-        [
-            (query_groups.shape, jnp.float32),
-            (key_groups.shape, jnp.bfloat16),
-            (value_groups.shape, jnp.bfloat16),
-        ],
-        "attend_back",
-    )
-    query_grad = jnp.transpose(query_grad, (0, 3, 1, 2, 4)).reshape(row_count, HEADS, HD)
-    pack_kv_grad = jnp.transpose(jnp.stack([key_grad, value_grad]), (1, 3, 0, 2, 4))
-    pack_kv_grad = pack_kv_grad.reshape(micro_count, -1, 2 * kv_width)
-    local_kv_grad = (
-        lax.psum_scatter(pack_kv_grad, "ctx", scatter_dimension=1, tiled=True)
-        .astype(jnp.float32)
-        .reshape(row_count, 2 * kv_width)
-    )
-    query_pre = rotate_back(query_grad, local_pos).reshape(row_count, HEADS * HD)
-    key_pre = rotate_back(
-        local_kv_grad[:, :kv_width].reshape(row_count, KV, HD), local_pos
-    ).reshape(row_count, kv_width)
-    projected_grad = jnp.concatenate([query_pre, key_pre, local_kv_grad[:, kv_width:]], -1).astype(
-        jnp.bfloat16
-    )
-    normed_grad = times_transposed(projected_grad, qkv_weight)
+    queries, packs, log_parts = parts
+    query_grads, kv_grads = [], []
+    for micro in range(micro_count):
+        rows = slice(micro * count, (micro + 1) * count)
+        query_part, kv_part = local_call(
+            attend_back_kernel,
+            (queries[rows], packs[micro], mixed_grad[rows], log_parts[micro]) + masks[micro],
+            [((count, HEADS * HD), jnp.float32), (packs[micro].shape, jnp.bfloat16)],
+            "attend_back",
+        )
+        query_grads.append(query_part)
+        kv_grads.append(lax.psum_scatter(kv_part, "ctx", scatter_dimension=0, tiled=True))
+    projected_grad = unturn(
+        jnp.concatenate(query_grads, 0), jnp.concatenate(kv_grads, 0), *turns
+    )
+    normed_grad = times_transposed(projected_grad, qkv_weight[:, : projected_grad.shape[1]])
     _, pull_one = jax.vjp(norm_scale, hidden, gain_pair[0])
     hidden_part, gain_one_grad = pull_one(normed_grad)
     input_grad = attended_grad + hidden_part
@@ -517,7 +525,7 @@
     gain_pair = fulls[0][:, qkv_width : qkv_width + 2].T.astype(jnp.float32)
     weights = (
         gain_pair,
-        fulls[0][:, :qkv_width],
+        fulls[0],
         fulls[1],
         jnp.concatenate([fulls[2], fulls[3]], -1),
         fulls[4],
@@ -527,19 +535,30 @@
     seg_q = lax.dynamic_slice_in_dim(seg_k, offset, token_count, 1)
     local_pos = lax.dynamic_slice_in_dim(pos_k, offset, token_count, 1).reshape(row_count)
     place = offset + jnp.arange(token_count, dtype=jnp.int32)
-    masks = (seg_q[:, :, None], seg_k[:, None, :], place[:, None])
+    masks = [
+        (seg_q[micro][:, None], seg_k[micro][None, :], place[:, None])
+        for micro in range(micro_count)
+    ]
+    half = HD // 2
+    frequency = ROPE_BASE ** (-(jnp.arange(half, dtype=jnp.float32) * 2.0 / HD))
+    angles = local_pos[:, None] * frequency[None, :]
+    cosine, sine = jnp.cos(angles), jnp.sin(angles)
+    turns = (
+        jnp.concatenate([cosine] * 4, -1),
+        jnp.concatenate([-sine, sine, -sine, sine], -1),
+    )
 
     first_input = tokens.reshape(row_count, width)
-    first_result, _ = layer_forward(first_input, masks, local_pos, weights, micro_count)
+    first_result, _ = layer_forward(first_input, masks, turns, weights, micro_count)
     incoming = shifted(first_result, "section", 1)
     hidden_in = jnp.where(section_index == 0, first_input, incoming)
-    result, saved = layer_forward(hidden_in, masks, local_pos, weights, micro_count)
+    result, saved = layer_forward(hidden_in, masks, turns, weights, micro_count)
     given = cotangent.reshape(row_count, width).astype(jnp.float32)
-    last_grad, _ = layer_backward(given, saved, masks, local_pos, weights, micro_count)
+    last_grad, _ = layer_backward(given, saved, masks, turns, weights, micro_count)
     incoming_grad = shifted(last_grad.astype(jnp.bfloat16), "section", -1)
     upstream = jnp.where(section_index == 1, given, incoming_grad.astype(jnp.float32))
     input_grad, weight_grads = layer_backward(
-        upstream, saved, masks, local_pos, weights, micro_count
+        upstream, saved, masks, turns, weights, micro_count
     )
     gain_one, gain_two, grad_qkv, grad_out, grad_gate_up, grad_down = weight_grads()
     spare_columns = jnp.zeros((width, spare), jnp.float32)

time: 554 us -> 523 us (0.944)
  blocking collectives: 0 us -> 78 us
  local copies, waits for them, and re-layouts: 117 us -> 56.6 us
  waiting for transfers between devices: 112 us -> 58.7 us
  Pallas kernels: 216 us -> 232 us
  other arithmetic: 31.2 us -> 18.8 us
    all_gather x0 -> x4, blocking collectives: none -> 78 us  [layer_forward(): packs.append(lax.all_gather(local_kv[rows], 'ctx', axis=0, tiled=True))]
    all_gather x2 -> x0, waiting for transfers between devices: 59.3 us -> none  [layer_forward(): lax.all_gather(local_kv.reshape(micro_count, -1, 2 * kv_width), 'ctx', ax...]
    reshape x12 -> x0, local copies, waits for them, and re-layouts: 32.7 us -> none  [the longest x4 9.69 us: group_heads(): rows = values.reshape(micro_count, -1, KV, HEADS // KV, HD)]
    transpose x6 -> x0, local copies, waits for them, and re-layouts: 21.9 us -> none  [the longest x2 8.6 us: layer_backward(): jnp.transpose(jnp.stack([key_grad, value_grad]), (1, 3, 0, 2, 4))]
    pallas_call x4 -> x12, Pallas kernels: 79.4 us -> 93.2 us  [the longest x8 77.4 us: local_call(): pl.pallas_call(kernel, out_shape=[jax.ShapeDtypeStruct(shape, kind) for s...]
    reduce_scatter x2 -> x4, waiting for transfers between devices: 24.3 us -> 36.5 us  [layer_backward(): lax.psum_scatter(kv_part, 'ctx', scatter_dimension=0, tiled=True)]
    transpose x4 -> x0, other arithmetic: 12.1 us -> none  [the longest x2 8.63 us: layer_backward(): jnp.transpose(jnp.stack([key_grad, value_grad]), (1, 3, 0, 2, 4))]
    ppermute x2, waiting for transfers between devices: 28.4 us -> 22.1 us  [shifted(): lax.ppermute(value, axis, [(source, source + steps) for source in range(l...]
  transfers between devices with their start and end apart: 6 -> 6, of which waited for: 5 -> 5; matrix products, arithmetic and copies ran while one was open for 13% -> 7% of each run, Pallas kernels for 0% -> 5%
where the time goes in v2:
time: 523 us; the launch traced here: 516 us
  Pallas kernels  232 us (44%)
  blocking collectives  78 us (15%)
  waiting for transfers between devices  58.7 us (11%)
  local copies, waits for them, and re-layouts  56.6 us (11%)
  matrix products  51.8 us (10%)
  other arithmetic  18.8 us (4%)
  between operations  14.8 us (3%)
  starting transfers between devices  5.7 us (1%)
    all_gather x4, blocking collectives, layer_forward(): packs.append(lax.all_gather(local_kv[rows], 'ctx', axis=0, tiled=True))  78 us
    pallas_call x8, Pallas kernels, local_call(): pl.pallas_call(kernel, out_shape=[jax.ShapeDtypeStruct(shape, kind) for s...  77.4 us
    pallas_call x1, Pallas kernels, reduce_parts(): pl.pallas_call(partial(reduce_kernel, fsdp_count, ctx_count, chunk_count)...  69.5 us
    pallas_call x1, Pallas kernels, gather_shards(): pl.pallas_call(partial(gather_kernel, fsdp_count, ctx_count, chunk_count)...  69.1 us
    reduce_scatter x4, waiting for transfers between devices, layer_backward(): lax.psum_scatter(kv_part, 'ctx', scatter_dimension=0, tiled=True)  36.5 us
    ppermute x2, waiting for transfers between devices, shifted(): lax.ppermute(value, axis, [(source, source + steps) for source in range(l...  22.1 us
    dot_general x8, matrix products, times_transposed(): lax.dot_general(left_side, right_side, (((1,), (1,)), ((), ())), preferre...  21.5 us
    dot_general x6, matrix products, matmul(): return jnp.dot(left_side, right_side, preferred_element_type=jnp.float32)  17 us
  transfers between devices with their start and end apart: 6, of which 5 were waited for; matrix products, arithmetic and copies ran while one was open for 7% of the time, Pallas kernels for 5%

profile of v2, /device:TPU:0, one launch (start us, length us, event | category | flops | bytes accessed | tf_op | source)
XLA Modules:
  0.0 516.1 jit_solution(15735376278831195749)
XLA Ops:
  16.4 69.1 %gather_weights.1 = (bf16[4,4,36,1024]{3,2,1,0:T(8,128)(2,1)}, bf16[4,4,36,576]{3,2,1,0:T(8,128)(2,1)}, bf16[4,4,36,1536]{3,2,1,0:T(8,128)(2,1)}, bf16[4,4,36,15...) custom-call(bf16[36,1024]{1,0:T(8,128)(2,1)} %maximum_maximum_fusion.1.refs_0_, bf16[36,576]{1,0:T(8,128)(2,1)} %bitcast.78, ...), custom_call_target="tpu_custom_call" | custom-call | tf_op jit(solution)/shard_map/gather_weights/pallas_call | solution.py:165
  96.8 24.0 %all_gather.12.kv_ref = bf16[1024,384]{1,0:T(8,128)(2,1)} all-gather(bf16[256,384]{1,0:T(8,128)(2,1)S(1)} %get-tuple-element.133), channel_id=1, replica_groups=mesh['section'=2,'fsdp'=4,'ctx'=4] {'ctx'}, dimensions={0}, use_global_device_ids=true | all-gather | bytes 983040 | tf_op jit(solution)/shard_map/all_gather | solution.py:428
  120.8 18.5 %all_gather.13.kv_ref = bf16[1024,384]{1,0:T(8,128)(2,1)} all-gather(bf16[256,384]{1,0:T(8,128)(2,1)S(1)} %get-tuple-element.134), channel_id=1, replica_groups=mesh['section'=2,'fsdp'=4,'ctx'=4] {'ctx'}, dimensions={0}, use_global_device_ids=true | all-gather | bytes 983040 | tf_op jit(solution)/shard_map/all_gather | solution.py:428
  139.3 7.3 %attend.4 = (bf16[256,576]{1,0:T(8,128)(2,1)}, f32[256,9]{1,0:T(8,128)}) custom-call(bf16[256,576]{1,0:T(8,128)(2,1)} %get-tuple-element.129.q_ref, bf16[1024,384]{1,0:T(8,128)(2,1)} %all_gather.12.kv_ref, s32[256,1]{1,0:T(8,128)} %copy.158.seg_q_ref, s32[1,1024]{1,0:T(1,128)} %get-tuple-element.137.seg_k_ref, s32[256,1]{1,0:T(8,128)} %iota_add_fusion.place_ref), custom_call_target="tpu_custom_call" | custom-call | flops 4000000000 | bytes 8000000 | tf_op jit(solution)/shard_map/attend/pallas_call | solution.py:409
  146.6 7.3 %attend.5 = (bf16[256,576]{1,0:T(8,128)(2,1)}, f32[256,9]{1,0:T(8,128)}) custom-call(bf16[256,576]{1,0:T(8,128)(2,1)} %get-tuple-element.130.q_ref, bf16[1024,384]{1,0:T(8,128)(2,1)} %all_gather.13.kv_ref, s32[256,1]{1,0:T(8,128)} %copy.159.seg_q_ref, s32[1,1024]{1,0:T(1,128)} %get-tuple-element.138.seg_k_ref, s32[256,1]{1,0:T(8,128)} %iota_add_fusion.place_ref), custom_call_target="tpu_custom_call" | custom-call | flops 4000000000 | bytes 8000000 | tf_op jit(solution)/shard_map/attend/pallas_call | solution.py:409
  165.2 4.8 fusion.26
  171.7 4.2 collective-permute-start
  176.2 7.8 %collective-permute-done = bf16[512,576]{0,1:T(8,128)(2,1)} collective-permute-done((bf16[512,576]{0,1:T(8,128)(2,1)S(1)}, bf16[512,576]{0,1:T(8,128)(2,1)}, u32[]{:S(2)}, u32[]{:S(2)}) %collective-permute-start) | collective-permute-done | bytes 589856 | tf_op jit(solution)/shard_map/ppermute | solution.py:24
  186.3 4.2 project.3
  192.5 17.6 %all_gather.15.kv_ref = bf16[1024,384]{1,0:T(8,128)(2,1)} all-gather(bf16[256,384]{1,0:T(8,128)(2,1)S(1)} %get-tuple-element.131), channel_id=1, replica_groups=mesh['section'=2,'fsdp'=4,'ctx'=4] {'ctx'}, dimensions={0}, use_global_device_ids=true | all-gather | bytes 983040 | tf_op jit(solution)/shard_map/all_gather | solution.py:428
  210.2 17.9 %all_gather.14.kv_ref = bf16[1024,384]{1,0:T(8,128)(2,1)} all-gather(bf16[256,384]{1,0:T(8,128)(2,1)S(1)} %get-tuple-element.132), channel_id=1, replica_groups=mesh['section'=2,'fsdp'=4,'ctx'=4] {'ctx'}, dimensions={0}, use_global_device_ids=true | all-gather | bytes 983040 | tf_op jit(solution)/shard_map/all_gather | solution.py:428
  228.0 7.2 %attend.6 = (bf16[256,576]{1,0:T(8,128)(2,1)}, f32[256,9]{1,0:T(8,128)}) custom-call(bf16[256,576]{1,0:T(8,128)(2,1)} %get-tuple-element.128.q_ref, bf16[1024,384]{1,0:T(8,128)(2,1)} %all_gather.14.kv_ref, s32[256,1]{1,0:T(8,128)} %copy.158.seg_q_ref, s32[1,1024]{1,0:T(1,128)} %get-tuple-element.137.seg_k_ref, s32[256,1]{1,0:T(8,128)} %iota_add_fusion.place_ref), custom_call_target="tpu_custom_call" | custom-call | flops 4000000000 | bytes 8000000 | tf_op jit(solution)/shard_map/attend/pallas_call | solution.py:409
  236.3 7.3 %attend.7 = (bf16[256,576]{1,0:T(8,128)(2,1)}, f32[256,9]{1,0:T(8,128)}) custom-call(bf16[256,576]{1,0:T(8,128)(2,1)} %get-tuple-element.127.q_ref, bf16[1024,384]{1,0:T(8,128)(2,1)} %all_gather.15.kv_ref, s32[256,1]{1,0:T(8,128)} %copy.159.seg_q_ref, s32[1,1024]{1,0:T(1,128)} %get-tuple-element.138.seg_k_ref, s32[256,1]{1,0:T(8,128)} %iota_add_fusion.place_ref), custom_call_target="tpu_custom_call" | custom-call | flops 4000000000 | bytes 8000000 | tf_op jit(solution)/shard_map/attend/pallas_call | solution.py:409
  256.0 12.2 %attend_back.4 = (f32[256,576]{1,0:T(8,128)}, bf16[1024,384]{1,0:T(8,128)(2,1)}) custom-call(bf16[256,576]{1,0:T(8,128)(2,1)} %get-tuple-element.128.q_ref, bf16[1024,384]{1,0:T(8,128)(2,1)} %all_gather.14.kv_ref, bf16[256,576]{1,0:T(8,128)(2,1)} %get-tuple-element.125.go_ref, f32[256,9]{1,0:T(8,128)} %get-tuple-element.50.log_ref, ...), custom_call_target="tpu_custom_call" | custom-call | flops 4000000000 | bytes 8000000 | tf_op jit(solution)/shard_map/attend_back/pallas_call | solution.py:409
  268.3 11.9 %attend_back.5 = (f32[256,576]{1,0:T(8,128)}, bf16[1024,384]{1,0:T(8,128)(2,1)}) custom-call(bf16[256,576]{1,0:T(8,128)(2,1)} %get-tuple-element.127.q_ref, bf16[1024,384]{1,0:T(8,128)(2,1)} %all_gather.15.kv_ref, bf16[256,576]{1,0:T(8,128)(2,1)} %get-tuple-element.126.go_ref, f32[256,9]{1,0:T(8,128)} %get-tuple-element.52.log_ref, ...), custom_call_target="tpu_custom_call" | custom-call | flops 4000000000 | bytes 8000000 | tf_op jit(solution)/shard_map/attend_back/pallas_call | solution.py:409
  282.8 10.9 %reduce-scatter.5.cloned.1.call-done = bf16[256,384]{1,0:T(8,128)(2,1)} async-done(((bf16[1024,384]{1,0:T(8,128)(2,1)}), bf16[256,384]{1,0:T(8,128)(2,1)}) %reduce-scatter.5.cloned.1.call-update) | async-done | bytes 196624 | tf_op jit(solution)/shard_map/reduce_scatter | solution.py:482
  293.7 24.8 %reduce-scatter.7.cloned.1.call-done = bf16[256,384]{1,0:T(8,128)(2,1)} async-done(((bf16[1024,384]{1,0:T(8,128)(2,1)}), bf16[256,384]{1,0:T(8,128)(2,1)}) %reduce-scatter.7.cloned.1.call-update) | async-done | bytes 196624 | tf_op jit(solution)/shard_map/reduce_scatter | solution.py:482
  330.3 14.4 %collective-permute-done.1 = bf16[512,576]{0,1:T(8,128)(2,1)S(1)} collective-permute-done((bf16[512,576]{0,1:T(8,128)(2,1)S(1)}, bf16[512,576]{0,1:T(8,128)(2,1)S(1)}, u32[]{:S(2)}, u32[]{:S(2)}) %collective-permute-start.1) | collective-permute-done | bytes 589856 | tf_op jit(solution)/shard_map/ppermute | solution.py:24
  345.0 6.3 %fusion.53 = (f32[512,1536]{1,0:T(8,128)S(1)}, f32[512,1536]{1,0:T(8,128)S(1)}, bf16[512,1536]{1,0:T(8,128)(2,1)}) fusion(f32[512,3072]{1,0:T(8,128)} %copy-done.34, bf16[1536,576]{1,0:T(8,128)(2,1)} %bitcast.88, bf16[512,576]{1,0:T(8,128)(2,1)S(1)} %copy.176, bf16[512,576]{1,0:T(8,128)(2,1)S(1)} %bitcast.70, pred[]{:T(512)S(6)} %eq.23), kind=kOutput, calls=%fused_computation.125 | convolution fusion | flops 918159360 | bytes 17104896 | tf_op jit(solution)/shard_map/dot_general | solution.py:32
  356.3 12.3 %attend_back.6 = (f32[256,576]{1,0:T(8,128)}, bf16[1024,384]{1,0:T(8,128)(2,1)}) custom-call(bf16[256,576]{1,0:T(8,128)(2,1)} %get-tuple-element.128.q_ref, bf16[1024,384]{1,0:T(8,128)(2,1)} %all_gather.14.kv_ref, bf16[256,576]{1,0:T(8,128)(2,1)} %get-tuple-element.123.go_ref, f32[256,9]{1,0:T(8,128)} %get-tuple-element.50.log_ref, ...), custom_call_target="tpu_custom_call" | custom-call | flops 4000000000 | bytes 8000000 | tf_op jit(solution)/shard_map/attend_back/pallas_call | solution.py:409
  368.6 4.3 fusion.9
  380.2 11.9 %attend_back.7 = (f32[256,576]{1,0:T(8,128)}, bf16[1024,384]{1,0:T(8,128)(2,1)}) custom-call(bf16[256,576]{1,0:T(8,128)(2,1)} %get-tuple-element.127.q_ref, bf16[1024,384]{1,0:T(8,128)(2,1)} %all_gather.15.kv_ref, bf16[256,576]{1,0:T(8,128)(2,1)} %get-tuple-element.124.go_ref, f32[256,9]{1,0:T(8,128)} %get-tuple-element.52.log_ref, ...), custom_call_target="tpu_custom_call" | custom-call | flops 4000000000 | bytes 8000000 | tf_op jit(solution)/shard_map/attend_back/pallas_call | solution.py:409
  392.1 5.0 convolution_convert_fusion
  431.8 69.5 %reduce_grads.1 = (f32[36,1024]{1,0:T(8,128)}, f32[36,576]{1,0:T(8,128)}, f32[36,1536]{1,0:T(8,128)}, f32[36,1536]{1,0:T(8,128)}, f32[96,576]{1,0:T(8,128)}) custom-call(bf16[4,4,36,1024]{3,2,1,0:T(8,128)(2,1)} %maximum_maximum_fusion.refs_0_, bf16[4,4,36,576]{3,2,1,0:T(8,128)(2,1)} %reshape.151.refs_1_, bf16[4,4,36,1536]{3,2,1,0:T(8,128)(2,1)} %reshape.152.refs_2_, ...), custom_call_target="tpu_custom_call" | custom-call | tf_op jit(solution)/shard_map/reduce_grads/pallas_call | solution.py:280
  (182 shorter events, 120.6 us)
Async XLA Ops:
  7.2 7.3 %copy-start.22 = (bf16[2,256,576]{1,2,0:T(8,128)(2,1)S(1)}, bf16[2,256,576]{1,2,0:T(8,128)(2,1)}, u32[]{:S(2)}) copy-start(bf16[2,256,576]{1,2,0:T(8,128)(2,1)} %param.8) | copy-start | bytes 1769476
  7.2 8.5 %copy-start.30 = (bf16[1,36,960]{2,1,0:T(8,128)(2,1)S(1)}, bf16[1,36,960]{2,1,0:T(8,128)(2,1)}, u32[]{:S(2)}) copy-start(bf16[1,36,960]{2,1,0:T(8,128)(2,1)} %param.12) | copy-start | bytes 207364
  7.2 286.5 %reduce-scatter.5.cloned.1.call-start = ((), (), s32[]{:S(2)}) async-start(), calls=%async_computation.4 | async-start | bytes 983040 | tf_op jit(solution)/shard_map/reduce_scatter | solution.py:482
  146.6 7.3 %copy-start.7 = (bf16[2,256,576]{2,1,0:T(8,128)(2,1)S(1)}, bf16[2,256,576]{2,1,0:T(8,128)(2,1)}, u32[]{:S(2)}) copy-start(bf16[2,256,576]{2,1,0:T(8,128)(2,1)} %copy.152) | copy-start | bytes 1769476
  146.6 7.3 %copy-start.36 = (bf16[256,576]{1,0:T(8,128)(2,1)S(1)}, bf16[256,576]{1,0:T(8,128)(2,1)}, u32[]{:S(2)}) copy-start(bf16[256,576]{1,0:T(8,128)(2,1)} %get-tuple-element.40) | copy-start | bytes 884740
  165.2 4.8 copy-start.31
  171.4 4.5 copy-start.23
  171.7 12.3 %collective-permute-start = (bf16[512,576]{0,1:T(8,128)(2,1)S(1)}, bf16[512,576]{0,1:T(8,128)(2,1)}, u32[]{:S(2)}, u32[]{:S(2)}) collective-permute-start(bf16[512,576]{0,1:T(8,128)(2,1)S(1)} %copy.162), channel_id=1, source_target_pairs={{0,16},{1,17},{2,18},{3,19},{4,20},{5,21},{6,22},{7,23},{8,24},{9,... | collective-permute-start | bytes 1769480 | tf_op jit(solution)/shard_map/ppermute | solution.py:24
  176.2 72.4 %copy-start.8 = (bf16[2,256,576]{2,1,0:T(8,128)(2,1)}, bf16[2,256,576]{2,1,0:T(8,128)(2,1)S(1)}, u32[]{:S(2)}) copy-start(bf16[2,256,576]{2,1,0:T(8,128)(2,1)S(1)} %copy.168) | copy-start | bytes 1769476
  236.3 8.5 %copy-start = (bf16[512,576]{1,0:T(8,128)(2,1)S(1)}, bf16[512,576]{1,0:T(8,128)(2,1)}, u32[]{:S(2)}) copy-start(bf16[512,576]{1,0:T(8,128)(2,1)} %broadcast_select_fusion.h_ref) | copy-start | bytes 1769476
  244.8 3.8 copy-start.11
  245.6 8.3 %copy-start.1 = (f32[512,576]{1,0:T(8,128)}, f32[512,576]{1,0:T(8,128)S(1)}, u32[]{:S(2)}) copy-start(f32[512,576]{1,0:T(8,128)S(1)} %get-tuple-element.150) | copy-start | bytes 3538948
  268.2 50.3 %reduce-scatter.7.cloned.1.call-start = ((), (), s32[]{:S(2)}) async-start(), calls=%async_computation.5 | async-start | bytes 983040 | tf_op jit(solution)/shard_map/reduce_scatter | solution.py:482
  280.2 135.2 %reduce-scatter.9.cloned.1.call-start = ((), (), s32[]{:S(2)}) async-start(), calls=%async_computation.6 | async-start | bytes 983040 | tf_op jit(solution)/shard_map/reduce_scatter | solution.py:482
  329.0 15.7 %collective-permute-start.1 = (bf16[512,576]{0,1:T(8,128)(2,1)S(1)}, bf16[512,576]{0,1:T(8,128)(2,1)S(1)}, u32[]{:S(2)}, u32[]{:S(2)}) collective-permute-start(bf16[512,576]{0,1:T(8,128)(2,1)S(1)} %copy.175), channel_id=1, source_target_pairs={{16,0},{17,1},{18,2},{19,3},{20,4},{21,5},{22,6},{23,7},{24,8},{25... | collective-permute-start | bytes 1769480 | tf_op jit(solution)/shard_map/ppermute | solution.py:24
  344.9 6.3 %copy-start.12 = (bf16[512,576]{1,0:T(8,128)(2,1)}, bf16[512,576]{1,0:T(8,128)(2,1)S(1)}, u32[]{:S(2)}) copy-start(bf16[512,576]{1,0:T(8,128)(2,1)S(1)} %copy.176) | copy-start | bytes 1769476
  344.9 6.3 %copy-start.2 = (f32[512,576]{1,0:T(8,128)S(1)}, f32[512,576]{1,0:T(8,128)}, u32[]{:S(2)}) copy-start(f32[512,576]{1,0:T(8,128)} %copy-done.1) | copy-start | bytes 3538948
  345.0 6.3 %copy-start.18 = (bf16[576,3072]{1,0:T(8,128)(2,1)S(1)}, bf16[576,3072]{1,0:T(8,128)(2,1)}, u32[]{:S(2)}) copy-start(bf16[576,3072]{1,0:T(8,128)(2,1)} %constant_dynamic-update-slice_fusion) | copy-start | bytes 10616836
  356.3 12.4 %copy-start.3 = (f32[512,576]{1,0:T(8,128)S(1)}, f32[512,576]{1,0:T(8,128)}, u32[]{:S(2)}) copy-start(f32[512,576]{1,0:T(8,128)} %copy-done.1) | copy-start | bytes 3538948
  368.6 47.5 %reduce-scatter.11.cloned.1.call-start = ((), (), s32[]{:S(2)}) async-start(), calls=%async_computation.7 | async-start | bytes 983040 | tf_op jit(solution)/shard_map/reduce_scatter | solution.py:482
  399.1 3.8 copy-start.10
  399.1 3.9 copy-start.14
  417.9 3.7 copy-start.6
  431.8 72.0 %copy-start.15 = (f32[512,576]{1,0:T(8,128)S(1)}, f32[512,576]{1,0:T(8,128)}, u32[]{:S(2)}) copy-start(f32[512,576]{1,0:T(8,128)} %get-tuple-element.155) | copy-start | bytes 3538948
  (21 other events, 57.7 us)
Sparse Core Ops, SparseCore 0:
  268.4 25.3 reduce-scatter.4
  296.0 22.4 reduce-scatter.6
  368.7 22.6 reduce-scatter.8
  393.5 22.5 reduce-scatter.10
